TPU v7x, 32 devices: a whole 2x2x4 slice. The times are simulated.
32 devices in a mesh: gx: 4 (over x, core), gy: 2 (over y), gz: 4 (over z).
Axes of the slice: x: 2, y: 2, z: 4, core: 2. Of those that a mesh axis runs over, the one named last changes fastest.
Arguments:
- adjoint: float32 [19, 32, 32, 512], P(None, 'gx', 'gy', 'gz'), may hold values from -6 to 6
- density: float32 [2, 32, 32, 512], P(None, 'gx', 'gy', 'gz'), may hold values from 0.8 to 1.2
- velocity: float32 [2, 3, 32, 32, 512], P(None, None, 'gx', 'gy', 'gz'), may hold values from -0.25 to 0.25
- pore_mask: int32 [32, 32, 512], P('gx', 'gy', 'gz'), may hold values from 0 to 1, as said below
Outputs:
- adjoint_out: float32 [19, 32, 32, 512], P(None, 'gx', 'gy', 'gz')
- sensitivity: float32 [32, 32, 512], P('gx', 'gy', 'gz')
Inputs may be any that keep to these rules, and one draw needn't show every extreme that they name: `pore_mask`: 1 marks a pore voxel and 0 a solid one.
All inputs are finite; a program needn't handle non-finite values.
Results may differ from a plain program's by a relative error of at most 0.00002.
Values sent between devices are 32-bit elements; how exact they have to be, the bound alone decides.
No kernel may reach another device: no remote copies, remote signals or barrier semaphores. Data moves between devices by JAX's collectives and lax.ppermute only.
A program may use at most 128 MiB of HBM per device.

v0:
```python
import functools
import itertools

import jax
import jax.numpy as jnp
from jax import lax
from jax.experimental import pallas as pl
from jax.experimental.pallas import tpu as pltpu
from jax.sharding import PartitionSpec as P

VELOCITIES = [
    (0, 0, 0),
    (1, 0, 0),
    (-1, 0, 0),
    (0, 1, 0),
    (0, -1, 0),
    (0, 0, 1),
    (0, 0, -1),
    (1, 1, 0),
    (-1, -1, 0),
    (1, -1, 0),
    (-1, 1, 0),
    (1, 0, 1),
    (-1, 0, -1),
    (1, 0, -1),
    (-1, 0, 1),
    (0, 1, 1),
    (0, -1, -1),
    (0, 1, -1),
    (0, -1, 1),
]
OPPOSITE = [0, 2, 1, 4, 3, 6, 5, 8, 7, 10, 9, 12, 11, 14, 13, 16, 15, 18, 17]
OMEGA = 1.25
LANES = 128
GROUP = 16


def pops(axis, sign):
    return [j for j in range(19) if VELOCITIES[j][axis] == sign]


def mirrored(j):
    cx, cy, cz = VELOCITIES[j]
    return VELOCITIES.index((cx, cy, -cz))


Z_FLAT = pops(2, 0)
Z_UP = pops(2, 1)
Z_DOWN = [mirrored(j) for j in Z_UP]
RHO, UX, UY, UZ, KIND = range(5)
Z_PLACE = {("pop", j): (0, g) for g, j in enumerate(Z_FLAT[:8])}
Z_PLACE[("pop", Z_FLAT[8])] = (1, 5)
Z_PLACE[("field", RHO)] = (1, 6)
Z_PLACE[("field", KIND)] = (1, 7)
Z_PLACE[("field", UX)] = (2, 5)
Z_PLACE[("field", UY)] = (2, 6)
Z_PLACE[("field", UZ)] = (2, 7)
BELOW, ABOVE, OWN_LOW, OWN_HIGH, Z_TILES = 0, 3, 6, 7, 8


def face_lines(axis, toward):
    near = pops(axis, 0) + pops(axis, toward)
    lines = [("pop", j, 0) for j in near] + [("field", k, 0) for k in range(5)]
    return lines + [("pop", j, 1) for j in pops(axis, toward)]


def edge_lines(toward_x, toward_y):
    lines = [("field", k, 0, 0) for k in range(5)]
    for j in range(19):
        cx, cy, _ = VELOCITIES[j]
        if cx not in (0, toward_x) or cy not in (0, toward_y):
            continue
        lines.append(("pop", j, 0, 0))
        if cx:
            lines.append(("pop", j, 1, 0))
        if cy:
            lines.append(("pop", j, 0, 1))
        if cx and cy:
            lines.append(("pop", j, 1, 1))
    return lines


FACE = 24
EDGE = 24
SIDE = 15


def side_lines(axis, toward):
    full = [("pop", j) for j in pops(axis, toward)] + [("share", p) for p in range(5)]
    full += [("field", k) for k in (UX, UY, UZ, KIND)]
    ends = []
    for end in range(2):
        for j in pops(1 - axis, 1 - 2 * end):
            across = VELOCITIES[j][axis]
            if across in (0, toward):
                ends.append((j, abs(across), end))
    return full, ends


def lane_ids():
    return lax.broadcasted_iota(jnp.int32, (8, LANES), 1)


def field_of(refs, kind, index, at):
    adj, den, vel, mask = refs
    if kind == "pop":
        return adj[(index, *at)]
    if index == RHO:
        return den[(1, *at)]
    if index == KIND:
        return (mask[at] + 1).astype(jnp.float32)
    return vel[(1, index - UX, *at)]


def parity_of(axis):
    return lax.rem(lax.axis_index(axis), 2)


def on_side(parity, slot, act):
    @pl.when(parity == slot)
    def _():
        act(1)

    @pl.when(parity != slot)
    def _():
        act(0)


def has_partner(axis, slot):
    at = lax.axis_index(axis)
    to = at + jnp.where(lax.rem(at, 2) == slot, 1, -1)
    return (to >= 0) & (to < lax.axis_size(axis))


def pack_z_kernel(slots, adj_in, den_in, vel_in, mask_in, adj, den, vel, mask, near, *rest):
    packets, sems = rest[:slots], rest[slots]
    refs = (adj, den, vel, mask)
    ext_x, ext_y, _ = mask.shape
    starts = range(0, 19, 5)
    loads = [
        pltpu.make_async_copy(adj_in.at[start : min(start + 5, 19)], adj.at[start : min(start + 5, 19)], sems.at[at])
        for at, start in enumerate(starts)
    ] + [
        pltpu.make_async_copy(source, target, sems.at[len(starts) + at])
        for at, (source, target) in enumerate([(den_in, den), (vel_in, vel), (mask_in, mask)])
    ]
    for load in loads:
        load.start()
    lane = lane_ids()
    parity = parity_of("gz")
    parts = range(ext_y // 8)
    zero = jnp.zeros((8, LANES), jnp.float32)
    lows, highs = [[zero] * 3 for _ in parts], [[zero] * 3 for _ in parts]
    far_low, far_high = [zero for _ in parts], [zero for _ in parts]

    def gather(kind, index):
        for x, part in itertools.product(range(ext_x), parts):
            value = field_of(refs, kind, index, (x, pl.ds(8 * part, 8), slice(None)))
            if kind == "pop" and VELOCITIES[index][2] == 1:
                spot = GROUP * Z_UP.index(index) + 2 + x
                moved = pltpu.roll(value, spot, 1)
                lows[part][1] = jnp.where(lane == spot, moved, lows[part][1])
                far_low[part] = jnp.where(lane == spot + 1, moved, far_low[part])
            elif kind == "pop" and VELOCITIES[index][2] == -1:
                spot = GROUP * Z_DOWN.index(index) + 2 + x
                moved = pltpu.roll(value, spot, 1)
                highs[part][1] = jnp.where(lane == spot - 1, moved, highs[part][1])
                far_high[part] = jnp.where(lane == spot - 2, moved, far_high[part])
            else:
                tile, group = Z_PLACE[(kind, index)]
                spot = GROUP * group + 2 + x
                moved = pltpu.roll(value, spot, 1)
                lows[part][tile] = jnp.where(lane == spot, moved, lows[part][tile])
                highs[part][tile] = jnp.where(lane == spot - 1, moved, highs[part][tile])

    for start, load in zip(starts, loads):
        load.wait()
        for j in range(start, min(start + 5, 19)):
            gather("pop", j)
    for load in loads[len(starts) :]:
        load.wait()
    for k in range(5):
        gather("field", k)
    for part in parts:
        rows = pl.ds(8 * part, 8)
        low = lows[part]
        high = [pltpu.roll(tile, 1, 1) for tile in highs[part]]
        low[2] = jnp.where(lane < 5 * GROUP, pltpu.roll(far_low[part], LANES - 1, 1), low[2])
        high[2] = jnp.where(lane < 5 * GROUP, pltpu.roll(far_high[part], 2, 1), high[2])
        near[0, rows, :] = low[1]
        near[1, rows, :] = high[1]
        for slot in range(slots):
            there = has_partner("gz", slot)
            for tile in range(3):
                value = jnp.where(parity == slot, high[tile], low[tile])
                packets[slot][tile, rows, :] = jnp.where(there, value, 0.0)


def pack_lines(refs, first, packets, many_x, many_y, wanted, shares):
    to_x, y_lines = packets[:many_x], packets[many_x : many_x + many_y]
    to_xy = packets[many_x + many_y :]
    ext_x, ext_y, _ = refs[-1].shape
    every = slice(None)
    px, py = parity_of("gx"), parity_of("gy")

    def line_of(kind, index, x, y):
        if kind == "pop":
            return first[index, x + 2, y + 8 : y + 9, :]
        return field_of(refs, kind, index, (x, slice(y, y + 1), every))

    def pack_xy(slot_x, slot_y, side_x, side_y):
        packet = to_xy[many_x * slot_y + slot_x]
        for line, (kind, index, far_x, far_y) in enumerate(edge_lines(1 - 2 * side_x, 1 - 2 * side_y)):
            if wanted(kind, index):
                x = ext_x - 1 - far_x if side_x else far_x
                y = ext_y - 1 - far_y if side_y else far_y
                packet[line // 8, line % 8 : line % 8 + 1, :] = line_of(kind, index, x, y)

    def pack_y(slot, side):
        for line, (kind, index, depth) in enumerate(face_lines(1, 1 - 2 * side)):
            if wanted(kind, index):
                y = ext_y - 1 - depth if side else depth
                for x in range(ext_x):
                    y_lines[slot][line, x : x + 1, :] = line_of(kind, index, x, y)

    def pack_x(slot, side):
        full, ends = side_lines(0, 1 - 2 * side)
        for line, (kind, index) in enumerate(full):
            if kind == "field" and wanted(kind, index):
                to_x[slot][line] = field_of(refs, kind, index, (ext_x - 1 if side else 0, every, every))
            elif kind == "pop" and wanted(kind, index):
                to_x[slot][line] = first[index, (ext_x - 1 if side else 0) + 2, pl.ds(8, ext_y), :]
            elif kind == "share" and shares is not None:
                to_x[slot][line] = shares[side, index]
        for spot, (index, depth, end) in enumerate(ends):
            if wanted("pop", index):
                x = ext_x - 1 - depth if side else depth
                to_x[slot][SIDE - 1, spot : spot + 1, :] = line_of("pop", index, x, ext_y - 1 if end else 0)

    def when_there(there, packet, act):
        pl.when(there)(act)
        if shares is None:

            @pl.when(jnp.logical_not(there))
            def _():
                packet[...] = jnp.zeros(packet.shape, jnp.float32)

    for slot_y in range(many_y):
        there_y = has_partner("gy", slot_y)
        when_there(there_y, y_lines[slot_y], lambda: on_side(py, slot_y, functools.partial(pack_y, slot_y)))
        for slot_x in range(many_x):
            when_there(
                there_y & has_partner("gx", slot_x),
                to_xy[many_x * slot_y + slot_x],
                lambda: on_side(
                    py,
                    slot_y,
                    lambda side_y: on_side(px, slot_x, lambda side_x: pack_xy(slot_x, slot_y, side_x, side_y)),
                ),
            )
    for slot_x in range(many_x):
        when_there(
            has_partner("gx", slot_x), to_x[slot_x], lambda: on_side(px, slot_x, functools.partial(pack_x, slot_x))
        )


def is_flat(kind, index):
    return kind == "field" or VELOCITIES[index][2] == 0


def shift_kernel(slots, adj, den, vel, mask, first, *packets):
    many_x, many_y = slots
    _, ext_x, ext_y, _ = adj.shape
    for j in range(19):
        cz = VELOCITIES[j][2]
        for x, part in itertools.product(range(ext_x), range(ext_y // 8)):
            value = adj[j, x, pl.ds(8 * part, 8), :]
            first[j, 2 + x, pl.ds(8 + 8 * part, 8), :] = pltpu.roll(value, -cz % LANES, 1) if cz else value
    pack_lines((None, den, vel, mask), first, packets, many_x, many_y, is_flat, None)


def pack_xy_kernel(slots, den, vel, mask, near, *rest):
    many_x, many_y, many_z = slots
    count = many_x + many_y + many_x * many_y
    from_z, rest = rest[:many_z], rest[many_z + 1 + count :]
    z_set, first, packets, faces, shares = rest[0], rest[1], rest[2 : 2 + count], rest[-2], rest[-1]
    to_x, y_lines, to_xy = packets[:many_x], packets[many_x : many_x + many_y], packets[many_x + many_y :]
    to_y = rest[2 + count : -2]
    ext_x, ext_y = first.shape[1] - 4, near.shape[1]
    spot = lane_ids() % GROUP
    px, py, pz = parity_of("gx"), parity_of("gy"), parity_of("gz")

    z_set[OWN_LOW] = near[0]
    z_set[OWN_HIGH] = near[1]
    for tile in range(3):
        even = from_z[0][tile]
        odd = from_z[1][tile] if many_z > 1 else jnp.zeros_like(even)
        z_set[ABOVE + tile] = jnp.where(pz == 0, even, odd)
        z_set[BELOW + tile] = jnp.where(pz == 0, odd, even)

    for j in Z_UP + Z_DOWN:
        up = VELOCITIES[j][2] > 0
        group = (Z_UP if up else Z_DOWN).index(j)
        last = LANES - 1 if up else 0
        for part in range(ext_y // 8):
            halo = z_set[(ABOVE if up else BELOW) + 1, pl.ds(8 * part, 8), :]
            for x in range(ext_x):
                edge = pltpu.roll(halo, (last - 2 - GROUP * group - x) % LANES, 1)
                first[j, 2 + x, pl.ds(8 + 8 * part, 8), last : last + 1] = edge[:, last : last + 1]


    sub = lax.broadcasted_iota(jnp.int32, (8, LANES), 0)
    loaded = []
    for side, part in itertools.product(range(2), range(ext_y // 8)):
        toward, x = 1 - 2 * side, ext_x - 1 if side else 0
        pulled = []
        for j in range(19):
            cx, cy, _ = VELOCITIES[j]
            if cx == -toward:
                pulled.append(jnp.zeros((8, LANES), jnp.float32))
                continue
            value = first[j, x + 2 + cx, pl.ds(8 + 8 * part + cy, 8), :]
            if cy == -1 and part == 0:
                value = jnp.where(sub == 0, 0.0, value)
            if cy == 1 and part == ext_y // 8 - 1:
                value = jnp.where(sub == 7, 0.0, value)
            pulled.append(value)
        at = (x, pl.ds(8 * part, 8), slice(None))
        here = [den[(1, *at)], vel[(1, 0, *at)], vel[(1, 1, *at)], vel[(1, 2, *at)], mask[at] > 0]
        loaded.append((side, part, pulled, here))
    for side, part, pulled, (rho, ux, uy, uz, fluid) in loaded:
        wanted = pops(0, 1 - 2 * side)
        after, _ = collide(pulled, 1.0 / rho, rho, ux, uy, uz, None, wanted)
        for line, j in enumerate(wanted):
            shares[side, line, pl.ds(8 * part, 8), :] = jnp.where(fluid, after[j], 0.0)

    pack_lines((mask,), first, packets, many_x, many_y, lambda kind, index: not is_flat(kind, index), shares)

    for side in range(2):
        for part in range(ext_y // 8):
            rows = pl.ds(8 * part, 8)
            value = jnp.zeros((8, LANES), jnp.float32)
            for tile in range(Z_TILES):
                start = ext_x if side else 2
                moved = pltpu.roll(z_set[tile, rows, :], (2 * tile - start) % LANES, 1)
                value = jnp.where(spot // 2 == tile, moved, value)
            faces[side, rows, :] = value

    def add_xy(slot_x, slot_y, side_x, side_y):
        start = ext_y - 2 if side_y else 0
        to_xy[many_x * slot_y + slot_x][EDGE // 8, 0:2, :] = faces[side_x, start : start + 2, :]

    def add_y(slot, side):
        toward = 1 - 2 * side
        lines = {name: line for line, name in enumerate(face_lines(1, toward))}
        pulled = []
        for j in range(19):
            cx, cy, _ = VELOCITIES[j]
            if cy == -toward:
                pulled.append(jnp.zeros((8, LANES), jnp.float32))
                continue
            value = y_lines[slot][lines[("pop", j, abs(cy))]]
            if cx:
                value = jnp.where(sub == (7 if cx > 0 else 0), 0.0, pltpu.roll(value, -cx % 8, 0))
            pulled.append(value)
        rho, ux, uy, uz, kind = [y_lines[slot][lines[("field", k, 0)]] for k in range(5)]
        after, _ = collide(pulled, 1.0 / rho, rho, ux, uy, uz, None, pops(1, toward))
        full, ends = side_lines(1, toward)
        for line, (what, index) in enumerate(full):
            if what == "share":
                to_y[slot][line] = jnp.where(kind > 1.5, after[pops(1, toward)[index]], 0.0)
            else:
                to_y[slot][line] = y_lines[slot][lines[(what, index, 0)]]
        for spot, (index, depth, end) in enumerate(ends):
            x = ext_x - 1 if end else 0
            to_y[slot][SIDE - 1, spot : spot + 1, :] = y_lines[slot][lines[("pop", index, depth)], x : x + 1, :]
        start = ext_y - 2 if side else 0
        for tile in range(Z_TILES):
            row = 2 * tile % 8
            to_y[slot][SIDE + tile // 4, row : row + 2, :] = z_set[tile, start : start + 2, :]

    def add_x(slot, side):
        to_x[slot][SIDE] = faces[side]

    for slot_y in range(many_y):
        there_y = has_partner("gy", slot_y)
        pl.when(there_y)(lambda: on_side(py, slot_y, functools.partial(add_y, slot_y)))

        @pl.when(jnp.logical_not(there_y))
        def _():
            to_y[slot_y][...] = jnp.zeros(to_y[slot_y].shape, jnp.float32)

        for slot_x in range(many_x):
            pl.when(there_y & has_partner("gx", slot_x))(
                lambda: on_side(
                    py,
                    slot_y,
                    lambda side_y: on_side(px, slot_x, lambda side_x: add_xy(slot_x, slot_y, side_x, side_y)),
                )
            )
    for slot_x in range(many_x):
        pl.when(has_partner("gx", slot_x))(lambda: on_side(px, slot_x, functools.partial(add_x, slot_x)))


def collide(pulled, inverse, rho, ux, uy, uz, fluid, wanted):
    total = {}
    diff = {}
    for j in range(1, 19, 2):
        total[j] = pulled[j] + pulled[j + 1]
        diff[j] = pulled[j] - pulled[j + 1]
    in_xy, in_xz, in_yz = total[7] + total[9], total[11] + total[13], total[15] + total[17]
    two_x, two_y, two_z = total[1] + total[1], total[3] + total[3], total[5] + total[5]
    count = (12.0 * pulled[0] + (two_x + two_y)) + (two_z + (in_xy + (in_xz + in_yz)))
    flow_x = (diff[1] + diff[1]) + ((diff[7] + diff[9]) + (diff[11] + diff[13]))
    flow_y = (diff[3] + diff[3]) + ((diff[7] - diff[9]) + (diff[15] + diff[17]))
    flow_z = (diff[5] + diff[5]) + ((diff[11] - diff[13]) + (diff[15] - diff[17]))
    xx, yy, zz = two_x + (in_xy + in_xz), two_y + (in_xy + in_yz), two_z + (in_xz + in_yz)
    xy, xz, yz = total[7] - total[9], total[11] - total[13], total[15] - total[17]
    push_x = xx * ux + xy * uy + xz * uz
    push_y = xy * ux + yy * uy + yz * uz
    push_z = xz * ux + yz * uy + zz * uz
    usq = ux * ux + uy * uy + uz * uz
    push = ux * push_x + uy * push_y + uz * push_z
    base = count * (OMEGA / 36.0 + (OMEGA / 24.0) * usq) - (OMEGA / 8.0) * push - ux * inverse
    along_x = (OMEGA / 12.0) * (flow_x + 3.0 * push_x - ux * count) + inverse
    along_y = (OMEGA / 12.0) * (flow_y + 3.0 * push_y - uy * count)
    along_z = (OMEGA / 12.0) * (flow_z + 3.0 * push_z - uz * count)
    parts = {
        1: along_x,
        3: along_y,
        5: along_z,
        7: along_x + along_y,
        9: along_x - along_y,
        11: along_x + along_z,
        13: along_x - along_z,
        15: along_y + along_z,
        17: along_y - along_z,
    }
    out = {}
    for j in wanted:
        if j == 0:
            shift = base
        elif j % 2:
            shift = base + parts[j]
        else:
            shift = base - parts[j - 1]
        out[j] = (1.0 - OMEGA) * pulled[j] + shift
        if fluid is not None:
            out[j] = jnp.where(fluid, out[j], pulled[OPPOSITE[j]])
    change = (-1.0 / 6.0) * rho * (flow_x * ux + flow_y * uy + flow_z * uz)
    return out, change if fluid is None else jnp.where(fluid, change, 0.0)


def only(value, row):
    return jnp.where(lax.broadcasted_iota(jnp.int32, (8, LANES), 0) == row, value, 0.0)


class Plane:
    def rim(self, shares, line, toward):
        if toward != (-1 if self.row < 0 else 1):
            return 0.0
        return only(shares[line, self.x, pl.ds(8 + self.row, 8), :], 0 if toward < 0 else 1)

    def __init__(self, x, row):
        self.x, self.row = x, row

    def load(self, ref, lead, margin, cx=0, cy=0):
        return ref[lead, self.x + margin + cx, pl.ds(8 + self.row + cy, 8), :]

    def store(self, ref, lead, margin, value):
        ref[lead, self.x + margin, pl.ds(8 + self.row, 8), :] = value


class Rim:
    def __init__(self, x, ext_y):
        self.x, self.ext_y = x, ext_y

    def rim(self, shares, line, toward):
        start = 1 if toward < 0 else 8 + self.ext_y - 1
        return only(shares[line, self.x, pl.ds(start, 8), :], 6 if toward < 0 else 1)

    def load(self, ref, lead, margin, cx=0, cy=0):
        at = self.x + margin + cx
        upper = ref[lead, at, pl.ds(8 + self.ext_y - 1 + cy, 8), :]
        lower = ref[lead, at, pl.ds(1 + cy, 8), :]
        return jnp.where(lax.broadcasted_iota(jnp.int32, (8, LANES), 0) < 4, upper, lower)

    def store(self, ref, lead, margin, value):
        at = self.x + margin
        ref[lead, at, pl.ds(8 + self.ext_y - 1, 2), :] = value[0:2]
        ref[lead, at, pl.ds(7, 2), :] = value[6:8]


def first_step(first, fields, second, change, tiles, outside=True, shares=None, y_shares=None):
    loaded = [
        (
            [tile.load(first, j, 2, *VELOCITIES[j][:2]) for j in range(19)],
            [tile.load(fields, k, 1) for k in range(5)],
        )
        for tile in tiles
    ]
    done = [
        collide(pulled, 1.0 / rho, rho, ux, uy, uz, kind > 1.5, range(19))
        for pulled, (rho, ux, uy, uz, kind) in loaded
    ]
    for tile, (_, here), (after, gain) in zip(tiles, loaded, done):
        inside = here[KIND] > 0.5
        side = None if shares is None else {-1: 0, second.shape[1] - 2: 1}.get(tile.x)
        for j in range(19):
            value = after[j]
            if side is not None and VELOCITIES[j][0] == 2 * side - 1:
                value = value + shares[side, pops(0, 2 * side - 1).index(j), pl.ds(8 + tile.row, 8), :]
            if side is None and y_shares is not None and VELOCITIES[j][1]:
                value = value + tile.rim(y_shares, pops(1, VELOCITIES[j][1]).index(j), VELOCITIES[j][1])
            if outside:
                value = jnp.where(inside, value, 0.0)
            cz = VELOCITIES[j][2]
            tile.store(second, j, 1, pltpu.roll(value, -cz % LANES, 1) if cz else value)
        tile.store(change, 0, 1, gain)


def inner_kernel(den, vel, mask, first, fields, second, change):
    refs = (None, den, vel, mask)
    ext_x, ext_y, _ = mask.shape
    every = slice(None)
    for k in range(5):
        fields[k, 1 : 1 + ext_x, pl.ds(8, ext_y), :] = field_of(refs, "field", k, (every, every, every))

    many = 3 if (ext_x - 2) % 3 == 0 else 1

    @pl.loop(0, (ext_x - 2) // many)
    def _(group):
        tiles = [Plane(many * group + at + 1, 1 + 8 * part) for at in range(many) for part in range(ext_y // 8)]
        first_step(first, fields, second, change, tiles, outside=False)


def put_row(first, fields, kind, index, x, y, value):
    row = y + 8
    if kind == "pop":
        first[index, x + 2, row : row + 1, :] = value
    else:
        fields[index, x + 1, row : row + 1, :] = value


def place_z(z_first, value, start, size, side, ext_x):
    rows = pl.ds(start, size)
    spot = lane_ids()[:size] % GROUP
    inside = spot >= 2 + ext_x if side else spot < 2
    for tile in range(Z_TILES):
        shift = (2 + ext_x if side else 0) - 2 * tile
        moved = pltpu.roll(value, shift % LANES, 1)[:size]
        z_first[tile, rows, :] = jnp.where(inside, moved, z_first[tile, rows, :])


def side_kernel(slots, z_set, *rest):
    many_x, many_y = slots
    from_x, from_y = rest[4 : 4 + many_x], rest[4 + many_x : 4 + many_x + many_y]
    first, fields, second, change, z_first, shares, y_shares = rest[-7:]
    _, ext_y, _ = z_set.shape
    ext_x = change.shape[1] - 2
    inner = pl.ds(8, ext_y)
    put = functools.partial(put_row, first, fields)
    z_first[:, inner, :] = z_set[...]

    def place_y(slot, side):
        packet = from_y[slot]
        toward = 2 * side - 1
        near = ext_y if side else -1
        nothing = jnp.zeros((1, LANES), jnp.float32)
        full, ends = side_lines(1, toward)
        for x in range(ext_x):
            for j in pops(1, 0):
                put("pop", j, x, near, nothing)
            for j in pops(1, toward):
                put("pop", j, x, near + toward, nothing)
            put("field", RHO, x, near, jnp.full((1, LANES), jnp.inf, jnp.float32))
            for line, (kind, index) in enumerate(full):
                if kind == "share":
                    y_shares[index, x, near + 8 : near + 9, :] = packet[line, x : x + 1, :]
                else:
                    put(kind, index, x, near, packet[line, x : x + 1, :])
        for spot, (index, depth, end) in enumerate(ends):
            put("pop", index, ext_x - 1 if end else 0, near + toward * depth, packet[SIDE - 1, spot : spot + 1, :])
        start = 8 + ext_y if side else 6
        for tile in range(Z_TILES):
            row = 2 * tile % 8
            z_first[tile, start : start + 2, :] = packet[SIDE + tile // 4, row : row + 2, :]
        if many_y == 1:
            clear_y(1 - side)

    def clear_y(side):
        nothing = jnp.zeros((1, LANES), jnp.float32)
        y = ext_y if side else -1
        for x in range(-2, ext_x + 2):
            for j in pops(1, 2 * side - 1):
                put("pop", j, x, y, nothing)
        for x in range(-1, ext_x + 1):
            put("field", KIND, x, y, nothing)
        start = 8 + ext_y if side else 6
        for tile in range(Z_TILES):
            z_first[tile, start : start + 2, :] = jnp.zeros((2, LANES), jnp.float32)

    def place_x(slot, side):
        packet = from_x[slot]
        toward = 2 * side - 1
        near = ext_x if side else -1
        nothing = jnp.zeros((ext_y, LANES), jnp.float32)
        for j in pops(0, 0):
            first[j, near + 2, inner, :] = nothing
        for j in pops(0, toward):
            first[j, near + toward + 2, inner, :] = nothing
        fields[RHO, near + 1, inner, :] = jnp.full((ext_y, LANES), jnp.inf, jnp.float32)
        full, ends = side_lines(0, toward)
        for line, (kind, index) in enumerate(full):
            if kind == "pop":
                first[index, near + 2, inner, :] = packet[line]
            elif kind == "share":
                shares[side, index, inner, :] = packet[line]
            else:
                fields[index, near + 1, inner, :] = packet[line]
        for spot, (index, depth, end) in enumerate(ends):
            put("pop", index, near + toward * depth, ext_y - 1 if end else 0, packet[SIDE - 1, spot : spot + 1, :])
        for part in range(ext_y // 8):
            place_z(z_first, packet[SIDE, pl.ds(8 * part, 8), :], 8 + 8 * part, 8, side, ext_x)

    shares[:, :, pl.ds(0, 8), :] = jnp.zeros((2, 5, 8, LANES), jnp.float32)
    shares[:, :, pl.ds(8 + ext_y, 8), :] = jnp.zeros((2, 5, 8, LANES), jnp.float32)
    for slot_y in range(many_y):
        on_side(parity_of("gy"), slot_y, functools.partial(place_y, slot_y))
    for slot_x in range(many_x):
        on_side(parity_of("gx"), slot_x, functools.partial(place_x, slot_x))

    rims = range(7, ext_y - 8, 8)
    first_step(first, fields, second, change, [Plane(x, row) for x in (0, ext_x - 1) for row in rims], outside=False)
    first_step(first, fields, second, change, [Plane(x, row) for x in (-1, ext_x) for row in rims], shares=shares)

    many = 3 if (ext_x - 2) % 3 == 0 else 1

    @pl.loop(0, (ext_x - 2) // many)
    def _(group):
        tiles = [Rim(many * group + at + 1, ext_y) for at in range(many)]
        first_step(first, fields, second, change, tiles, y_shares=y_shares)


def last_kernel(slots, den, vel, mask, *rest):
    many_x, many_y = slots
    from_xy = rest[7 : 7 + many_x * many_y]
    out, sens, first, fields, second, change, z_first, shares, y_shares = rest[-13:-4]
    z_second, held, held_sens, sems = rest[-4:]
    ext_x, ext_y, _ = mask.shape
    lane = lane_ids()
    every = slice(None)
    px, py = parity_of("gx"), parity_of("gy")

    def place_xy(slot_x, slot_y, side_x, side_y):
        packet = from_xy[many_x * slot_y + slot_x]
        for line, (kind, index, far_x, far_y) in enumerate(edge_lines(2 * side_x - 1, 2 * side_y - 1)):
            x = ext_x + far_x if side_x else -1 - far_x
            y = ext_y + far_y if side_y else -1 - far_y
            put_row(first, fields, kind, index, x, y, packet[line // 8, line % 8 : line % 8 + 1, :])
        place_z(z_first, packet[EDGE // 8], 8 + ext_y if side_y else 6, 2, side_x, ext_x)

    for slot_x in range(many_x):
        for slot_y in range(many_y):
            on_side(
                py,
                slot_y,
                lambda side_y: on_side(px, slot_x, lambda side_x: place_xy(slot_x, slot_y, side_x, side_y)),
            )

    for pair in ((-1, 0), (ext_x - 1, ext_x)):
        tiles = [Plane(x, row) for x in pair for row in (-1, ext_y - 1)]
        first_step(first, fields, second, change, tiles, shares=shares, y_shares=y_shares)

    starts = [7 + 8 * part for part in range((ext_y + 2 + 7) // 8)]
    loaded = []
    for row in starts:

        def both(low_tile, high_tile, group, cx, cy):
            rows = pl.ds(row + cy, 8)
            low = pltpu.roll(z_first[low_tile, rows, :], (-GROUP * group - cx) % LANES, 1)
            high = pltpu.roll(z_first[high_tile, rows, :], (LANES // 2 - GROUP * group - cx) % LANES, 1)
            return jnp.where(lane < LANES // 2, low, high)

        pulled = []
        for j in range(19):
            cx, cy, cz = VELOCITIES[j]
            if cz == 0:
                tile, group = Z_PLACE[("pop", j)]
                pulled.append(both(BELOW + tile, ABOVE + tile, group, cx, cy))
            elif cz == 1:
                pulled.append(both(OWN_LOW, ABOVE + 2, Z_UP.index(j), cx, cy))
            else:
                pulled.append(both(BELOW + 2, OWN_HIGH, Z_DOWN.index(j), cx, cy))
        places = [Z_PLACE[("field", k)] for k in range(5)]
        loaded.append((pulled, [both(BELOW + tile, ABOVE + tile, group, 0, 0) for tile, group in places]))
    done = [
        collide(pulled, 1.0 / rho, rho, ux, uy, uz, kind > 1.5, Z_UP + Z_DOWN)[0]
        for pulled, (rho, ux, uy, uz, kind) in loaded
    ]
    for row, (_, here), after in zip(starts, loaded, done):
        for group in range(5):
            value = jnp.where(lane < LANES // 2, after[Z_DOWN[group]], after[Z_UP[group]])
            z_second[group, pl.ds(row, 8), :] = jnp.where(here[KIND] > 0.5, value, 0.0)

    def copies(x):
        return (
            pltpu.make_async_copy(held.at[:, x], out.at[:, x], sems.at[0, x]),
            pltpu.make_async_copy(held_sens.at[x], sens.at[x], sems.at[1, x]),
        )

    many = 4 if ext_x % 4 == 0 else 1

    @pl.loop(0, ext_x // many)
    def _(group):
        loaded = []
        planes = [many * group + at for at in range(many)]
        for x, part in itertools.product(planes, range(ext_y // 8)):
            row = 8 + 8 * part
            pulled = []
            for j in range(19):
                cx, cy, cz = VELOCITIES[j]
                rows = pl.ds(row + cy, 8)
                value = second[j, x + 1 + cx, rows, :]
                if cz == 1:
                    edge = z_second[Z_UP.index(j), rows, :]
                    edge = pltpu.roll(edge, LANES // 2 - 3 - cx - x, 1)
                    value = jnp.where(lane == LANES - 1, edge, value)
                elif cz == -1:
                    edge = z_second[Z_DOWN.index(j), rows, :]
                    edge = pltpu.roll(edge, LANES - 2 - cx - x, 1)
                    value = jnp.where(lane == 0, edge, value)
                pulled.append(value)
            at = (x, pl.ds(8 * part, 8), every)
            rho = den[(0, *at)]
            here = [1.0 / rho, rho, vel[(0, 0, *at)], vel[(0, 1, *at)], vel[(0, 2, *at)], mask[at] > 0]
            loaded.append((at, pulled, here, change[0, x + 1, pl.ds(row, 8), :]))
        done = [collide(pulled, *here, range(19)) for _, pulled, here, _ in loaded]
        for (at, _, _, before), (after, gain) in zip(loaded, done):
            for j in range(19):
                held[(j, *at)] = after[j]
            held_sens[at] = before + gain
        for x in planes:
            for copy in copies(x):
                copy.start()

    for x in range(ext_x):
        for copy in copies(x):
            copy.wait()


def shards(adjoint, density, velocity, pore_mask):
    ext_x, ext_y, ext_z = pore_mask.shape
    assert ext_z == LANES and ext_y % 8 == 0 and ext_x + 4 <= GROUP and ext_x == 8
    many_x = 2
    many_y, many_z = [1 if lax.axis_size(axis) == 2 else 2 for axis in ("gy", "gz")]
    vmem = pl.BlockSpec(memory_space=pltpu.VMEM)
    hbm = pl.BlockSpec(memory_space=pltpu.HBM)
    inputs = (adjoint, density, velocity, pore_mask)

    def array(*shape):
        return jax.ShapeDtypeStruct(shape, jnp.float32)

    def call(kernel, name, operands, shapes, limit, **more):
        more.setdefault("out_specs", [vmem] * len(shapes))
        more.setdefault("in_specs", [vmem] * len(operands))
        params = pltpu.CompilerParams(vmem_limit_bytes=limit * 1024 * 1024)
        return pl.pallas_call(kernel, out_shape=shapes, compiler_params=params, name=name, **more)(*operands)

    def partners(axis, slot):
        found = {}
        for at in range(slot, lax.axis_size(axis) - 1, 2):
            found[at], found[at + 1] = at + 1, at
        return found

    def ends(axis):
        last = lax.axis_size(axis) - 1
        return {0: last, last: 0}

    def swap(value, spares, *places):
        tables = {axis: partners(axis, slot) for axis, slot in places}
        axes = [axis for axis in ("gx", "gy", "gz") if axis in tables or axis in dict(spares)]
        sizes = [lax.axis_size(axis) for axis in axes]
        pairs = []
        for at in itertools.product(*[range(size) for size in sizes]):
            to = [tables.get(axis, {}).get(spot, spot) for axis, spot in zip(axes, at)]
            for spare, table in spares:
                if tuple(to) == at:
                    to = [table.get(spot, spot) if axis == spare else spot for axis, spot in zip(axes, at)]
            flat = []
            for spots in (at, to):
                index = 0
                for size, spot in zip(sizes, spots):
                    index = index * size + spot
                flat.append(index)
            pairs.append(tuple(flat))
        return lax.ppermute(value, tuple(axes), pairs)

    loaded = [jax.ShapeDtypeStruct(value.shape, value.dtype) for value in inputs]
    *held, near, a_z, b_z = (
        *call(
            functools.partial(pack_z_kernel, many_z),
            "pack_z",
            [pltpu.with_memory_space_constraint(value, pltpu.HBM) for value in inputs],
            loaded + [array(2, ext_y, LANES)] + [array(3, ext_y, LANES)] * many_z,
            8,
            in_specs=[hbm] * 4,
            scratch_shapes=[pltpu.SemaphoreType.DMA((7,))],
        ),
        *[None] * (2 - many_z),
    )
    from_z = [swap(value, [("gx", partners("gx", 0))], ("gz", slot)) for slot, value in enumerate((a_z, b_z)[:many_z])]

    rows = ext_y + 16
    adj, den, vel, mask = held
    shapes = (
        [array(19, ext_x + 4, rows, LANES)]
        + [array(SIDE + 1, ext_y, LANES)] * many_x
        + [array(FACE, ext_x, LANES)] * many_y
        + [array(EDGE // 8 + 1, 8, LANES)] * (many_x * many_y)
    )
    shifted = call(
        functools.partial(shift_kernel, (many_x, many_y)),
        "shift",
        (adj, den, vel, mask),
        shapes,
        8,
        cost_estimate=pl.CostEstimate(flops=1_000_000, bytes_accessed=2_500_000, transcendentals=0),
    )
    z_set, first, *packets = call(
        functools.partial(pack_xy_kernel, (many_x, many_y, many_z)),
        "pack_xy",
        (den, vel, mask, near, *from_z, *shifted),
        [array(Z_TILES, ext_y, LANES)] + shapes + [array(SIDE + 2, ext_x, LANES)] * many_y,
        8,
        input_output_aliases={4 + many_z + at: 1 + at for at in range(len(shapes))},
        scratch_shapes=[
            pltpu.VMEM((2, ext_y, LANES), jnp.float32),
            pltpu.VMEM((2, 5, ext_y, LANES), jnp.float32),
        ],
    )
    to_x, to_xy, to_y = packets[:many_x], packets[many_x + many_y : -many_y], packets[-many_y:]
    from_xy = [
        swap(to_xy[many_x * slot_y + slot_x], [], ("gx", slot_x), ("gy", slot_y))
        for slot_y in range(many_y)
        for slot_x in range(many_x)
    ]
    from_y = [swap(value, [("gz", partners("gz", 0))], ("gy", slot)) for slot, value in enumerate(to_y)]
    spares = [("gx", ends("gx"))]
    if lax.axis_size("gz") > 2:
        top = lax.axis_size("gz") - 1
        spares = [("gz", {top - 1: top, top: top - 1})] + spares
    from_x = [swap(value, spares, ("gx", slot)) for slot, value in enumerate(to_x)]

    fields, second, change = call(
        inner_kernel,
        "inner_step",
        (den, vel, mask, first),
        [array(5, ext_x + 2, rows, LANES), array(19, ext_x + 2, rows, LANES), array(1, ext_x + 2, rows, LANES)],
        8,
        cost_estimate=pl.CostEstimate(flops=40_000_000, bytes_accessed=8_000_000, transcendentals=0),
    )
    inout = (first, fields, second, change)
    inout = call(
        functools.partial(side_kernel, (many_x, many_y)),
        "side_step",
        (z_set, *inout, *from_x, *from_y),
        [array(*value.shape) for value in inout] + [array(Z_TILES, rows, LANES), array(2, 5, rows, LANES), array(5, ext_x, rows, LANES)],
        8,
        input_output_aliases={1 + at: at for at in range(4)},
        cost_estimate=pl.CostEstimate(flops=40_000_000, bytes_accessed=8_000_000, transcendentals=0),
    )
    return call(
        functools.partial(last_kernel, (many_x, many_y)),
        "last_steps",
        (den, vel, mask, *inout, *from_xy),
        [array(19, ext_x, ext_y, LANES), array(ext_x, ext_y, LANES)] + [array(*value.shape) for value in inout],
        8,
        out_specs=[hbm] * 2 + [vmem] * 7,
        input_output_aliases={3 + at: 2 + at for at in range(7)},
        scratch_shapes=[
            pltpu.VMEM((5, rows, LANES), jnp.float32),
            pltpu.VMEM((19, ext_x, ext_y, LANES), jnp.float32),
            pltpu.VMEM((ext_x, ext_y, LANES), jnp.float32),
            pltpu.SemaphoreType.DMA((2, ext_x)),
        ],
    )[:2]


def solution(mesh):
    placed = (
        P(None, "gx", "gy", "gz"),
        P(None, "gx", "gy", "gz"),
        P(None, None, "gx", "gy", "gz"),
        P("gx", "gy", "gz"),
    )

    def whole(*arrays):
        return tuple(shards(*arrays))

    return jax.shard_map(
        whole,
        mesh=mesh,
        in_specs=placed,
        out_specs=(P(None, "gx", "gy", "gz"), P("gx", "gy", "gz")),
        check_vma=False,
    )
```

profile of v0, /device:TPU:9, one launch (start us, length us, event | category | flops | bytes accessed | tf_op | source)
XLA Modules:
  0.0 18.3 jit_solution(11977052767516673547)
XLA Ops:
  0.6 1.9 %pack_z.1 = (f32[19,8,16,128]{3,2,1,0:T(8,128)S(1)}, f32[2,8,16,128]{3,2,1,0:T(8,128)S(1)}, f32[2,3,8,16,128]{4,3,2,1,0:T(8,128)S(1)}, s32[8,16,128]{2,1,0:T(8,1...) custom-call(f32[19,8,16,128]{3,2,1,0:T(8,128)} %adj_in.1, ...), custom_call_target="tpu_custom_call" | custom-call | tf_op jit(solution)/shard_map/pack_z/pallas_call | solution.py:768
  2.5 0.1 collective-permute-start
  2.6 2.6 %collective-permute-start.1 = (f32[3,16,128]{2,1,0:T(8,128)S(1)}, f32[3,16,128]{2,1,0:T(8,128)S(1)}, u32[]{:S(2)}, u32[]{:S(2)}) collective-permute-start(f32[3,16,128]{2,1,0:T(8,128)S(1)} %get-tuple-element.39), channel_id=1, source_target_pairs={{0,8},{1,2},{2,1},{3,11},{8,0},{9,10},{10,9},{11,3},{16,24},{17,18... | collective-permute-start | bytes 73736 | tf_op jit(solution)/shard_map/ppermute | solution.py:797
  5.2 0.4 %shift.1 = (f32[19,12,32,128]{3,2,1,0:T(8,128)S(1)}, f32[16,16,128]{2,1,0:T(8,128)S(1)}, f32[16,16,128]{2,1,0:T(8,128)S(1)}, f32[24,8,128]{2,1,0:T(8,128)S(1)}, ...) custom-call(f32[19,8,16,128]{3,2,1,0:T(8,128)S(1)} %get-tuple-element.40.adj, ...), custom_call_target="tpu_custom_call" | custom-call | flops 1000000 | bytes 2500000 | tf_op jit(solution)/shard_map/shift/pallas_call | solution.py:768
  5.5 0.0 collective-permute-done.rest_0_
  5.5 1.1 %collective-permute-done.1.rest_1_ = f32[3,16,128]{2,1,0:T(8,128)S(1)} collective-permute-done((f32[3,16,128]{2,1,0:T(8,128)S(1)}, f32[3,16,128]{2,1,0:T(8,128)S(1)}, u32[]{:S(2)}, u32[]{:S(2)}) %collective-permute-start.1) | collective-permute-done | bytes 24608 | tf_op jit(solution)/shard_map/ppermute | solution.py:797
  6.7 0.5 %pack_xy.1 = (f32[8,16,128]{2,1,0:T(8,128)S(1)}, f32[19,12,32,128]{3,2,1,0:T(8,128)S(1)}, f32[16,16,128]{2,1,0:T(8,128)S(1)}, f32[16,16,128]{2,1,0:T(8,128)S(1)}...) custom-call(f32[2,8,16,128]{3,2,1,0:T(8,128)S(1)} %get-tuple-element, ...), custom_call_target="tpu_custom_call", output_to_operand_aliasing={{1}: (6, {}), {2}: (7, {}), {3}: (8, {}), {4}: (9, {}), {5}... | custom-call | tf_op jit(solution)/shard_map/pack_xy/pallas_call | solution.py:768
  7.2 1.6 %collective-permute-start.2 = (f32[16,16,128]{2,1,0:T(8,128)S(1)}, f32[16,16,128]{2,1,0:T(8,128)S(1)}, u32[]{:S(2)}, u32[]{:S(2)}) collective-permute-start(f32[16,16,128]{2,1,0:T(8,128)S(1)} %get-tuple-element.52), channel_id=1, source_target_pairs={{0,8},{1,9},{2,10},{3,11},{8,0},{9,1},{10,2},{11,3},{16,24},{17,25... | collective-permute-start | bytes 393224 | tf_op jit(solution)/shard_map/ppermute | solution.py:797
  8.7 1.2 %collective-permute-start.3 = (f32[16,16,128]{2,1,0:T(8,128)S(1)}, f32[16,16,128]{2,1,0:T(8,128)S(1)}, u32[]{:S(2)}, u32[]{:S(2)}) collective-permute-start(f32[16,16,128]{2,1,0:T(8,128)S(1)} %get-tuple-element.53), channel_id=1, source_target_pairs={{0,24},{1,25},{2,3},{3,2},{8,16},{9,17},{10,18},{11,19},{16,8},{17... | collective-permute-start | bytes 393224 | tf_op jit(solution)/shard_map/ppermute | solution.py:797
  10.0 1.2 %collective-permute-start.4 = (f32[17,8,128]{2,1,0:T(8,128)S(1)}, f32[17,8,128]{2,1,0:T(8,128)S(1)}, u32[]{:S(2)}, u32[]{:S(2)}) collective-permute-start(f32[17,8,128]{2,1,0:T(8,128)S(1)} %get-tuple-element.54), channel_id=1, source_target_pairs={{0,4},{1,5},{2,6},{3,7},{4,0},{5,1},{6,2},{7,3},{8,12},{9,13},{10,... | collective-permute-start | bytes 208904 | tf_op jit(solution)/shard_map/ppermute | solution.py:797
  11.2 0.8 %collective-permute-start.5 = (f32[4,8,128]{2,1,0:T(8,128)S(1)}, f32[4,8,128]{2,1,0:T(8,128)S(1)}, u32[]{:S(2)}, u32[]{:S(2)}) collective-permute-start(f32[4,8,128]{2,1,0:T(8,128)S(1)} %get-tuple-element.62), channel_id=1, source_target_pairs={{0,12},{4,8},{8,4},{12,0},{16,28},{20,24},{24,20},{28,16},{1,13},{... | collective-permute-start | bytes 49160 | tf_op jit(solution)/shard_map/ppermute | solution.py:797
  12.0 0.8 %collective-permute-start.6 = (f32[4,8,128]{2,1,0:T(8,128)S(1)}, f32[4,8,128]{2,1,0:T(8,128)S(1)}, u32[]{:S(2)}, u32[]{:S(2)}) collective-permute-start(f32[4,8,128]{2,1,0:T(8,128)S(1)} %get-tuple-element.63), channel_id=1, source_target_pairs={{0,4},{4,0},{8,20},{12,16},{16,12},{20,8},{24,28},{28,24},{1,5},{5... | collective-permute-start | bytes 49160 | tf_op jit(solution)/shard_map/ppermute | solution.py:797
  12.9 0.5 %inner_step.1 = (f32[5,10,32,128]{3,2,1,0:T(8,128)S(1)}, f32[19,10,32,128]{3,2,1,0:T(8,128)S(1)}, f32[1,10,32,128]{3,2,1,0:T(8,128)S(1)}) custom-call(f32[2,8,16,128]{3,2,1,0:T(8,128)S(1)} %get-tuple-element.34.den, f32[2,3,8,16,128]{4,3,2,1,0:T(8,128)S(1)} %get-tuple-element.35.vel, s32[8,16,128]{2,1,0:T(8,128)S(1)} %get-tuple-element.36.mask, ...), custom_call_target="tpu_custom_call" | custom-call | flops 40000000 | bytes 8000000 | tf_op jit(solution)/shard_map/inner_step/pallas_call | solution.py:768
  13.4 0.0 collective-permute-done.4.rest_6_
  13.4 0.0 collective-permute-done.2.rest_4_
  13.4 0.8 %collective-permute-done.3.rest_5_ = f32[16,16,128]{2,1,0:T(8,128)S(1)} collective-permute-done((f32[16,16,128]{2,1,0:T(8,128)S(1)}, f32[16,16,128]{2,1,0:T(8,128)S(1)}, u32[]{:S(2)}, u32[]{:S(2)}) %collective-permute-start.3) | collective-permute-done | bytes 131104 | tf_op jit(solution)/shard_map/ppermute | solution.py:797
  14.2 0.9 %side_step.1 = (f32[19,12,32,128]{3,2,1,0:T(8,128)S(1)}, f32[5,10,32,128]{3,2,1,0:T(8,128)S(1)}, f32[19,10,32,128]{3,2,1,0:T(8,128)S(1)}, f32[1,10,32,128]{3,2,1...) custom-call(f32[8,16,128]{2,1,0:T(8,128)S(1)} %get-tuple-element.47., ...), custom_call_target="tpu_custom_call", output_to_operand_aliasing={{0}: (1, {}), {1}: (2, {}), {2}: (3, {}), {3}: (4, {})} | custom-call | flops 40000000 | bytes 8000000 | tf_op jit(solution)/shard_map/side_step/pallas_call | solution.py:768
  15.1 0.0 collective-permute-done.5.rest_7_
  15.1 1.0 %collective-permute-done.6.rest_8_ = f32[4,8,128]{2,1,0:T(8,128)S(1)} collective-permute-done((f32[4,8,128]{2,1,0:T(8,128)S(1)}, f32[4,8,128]{2,1,0:T(8,128)S(1)}, u32[]{:S(2)}, u32[]{:S(2)}) %collective-permute-start.6) | collective-permute-done | bytes 16416 | tf_op jit(solution)/shard_map/ppermute | solution.py:797
  16.1 2.2 %last_steps.1 = (f32[19,8,16,128]{3,2,1,0:T(8,128)}, f32[8,16,128]{2,1,0:T(8,128)}, f32[19,12,32,128]{3,2,1,0:T(8,128)S(1)}, f32[5,10,32,128]{3,2,1,0:T(8,128)S(...) custom-call(f32[2,8,16,128]{3,2,1,0:T(8,128)S(1)} %get-tuple-element, ...), custom_call_target="tpu_custom_call", output_to_operand_aliasing={{2}: (3, {}), {3}: (4, {}), {4}: (5, {}), {5}: (6, {}), {6}... | custom-call | tf_op jit(solution)/shard_map/last_steps/pallas_call | solution.py:768
Async XLA Ops:
  2.5 3.0 %collective-permute-start = (f32[3,16,128]{2,1,0:T(8,128)S(1)}, f32[3,16,128]{2,1,0:T(8,128)S(1)}, u32[]{:S(2)}, u32[]{:S(2)}) collective-permute-start(f32[3,16,128]{2,1,0:T(8,128)S(1)} %get-tuple-element.38), channel_id=1, source_target_pairs={{0,1},{1,0},{2,3},{3,2},{8,9},{9,8},{10,11},{11,10},{16,17},{17,16... | collective-permute-start | bytes 73736 | tf_op jit(solution)/shard_map/ppermute | solution.py:797
  2.6 4.1 %collective-permute-start.1 = (f32[3,16,128]{2,1,0:T(8,128)S(1)}, f32[3,16,128]{2,1,0:T(8,128)S(1)}, u32[]{:S(2)}, u32[]{:S(2)}) collective-permute-start(f32[3,16,128]{2,1,0:T(8,128)S(1)} %get-tuple-element.39), channel_id=1, source_target_pairs={{0,8},{1,2},{2,1},{3,11},{8,0},{9,10},{10,9},{11,3},{16,24},{17,18... | collective-permute-start | bytes 73736 | tf_op jit(solution)/shard_map/ppermute | solution.py:797
  7.2 6.2 %collective-permute-start.2 = (f32[16,16,128]{2,1,0:T(8,128)S(1)}, f32[16,16,128]{2,1,0:T(8,128)S(1)}, u32[]{:S(2)}, u32[]{:S(2)}) collective-permute-start(f32[16,16,128]{2,1,0:T(8,128)S(1)} %get-tuple-element.52), channel_id=1, source_target_pairs={{0,8},{1,9},{2,10},{3,11},{8,0},{9,1},{10,2},{11,3},{16,24},{17,25... | collective-permute-start | bytes 393224 | tf_op jit(solution)/shard_map/ppermute | solution.py:797
  8.7 5.5 %collective-permute-start.3 = (f32[16,16,128]{2,1,0:T(8,128)S(1)}, f32[16,16,128]{2,1,0:T(8,128)S(1)}, u32[]{:S(2)}, u32[]{:S(2)}) collective-permute-start(f32[16,16,128]{2,1,0:T(8,128)S(1)} %get-tuple-element.53), channel_id=1, source_target_pairs={{0,24},{1,25},{2,3},{3,2},{8,16},{9,17},{10,18},{11,19},{16,8},{17... | collective-permute-start | bytes 393224 | tf_op jit(solution)/shard_map/ppermute | solution.py:797
  10.0 3.5 %collective-permute-start.4 = (f32[17,8,128]{2,1,0:T(8,128)S(1)}, f32[17,8,128]{2,1,0:T(8,128)S(1)}, u32[]{:S(2)}, u32[]{:S(2)}) collective-permute-start(f32[17,8,128]{2,1,0:T(8,128)S(1)} %get-tuple-element.54), channel_id=1, source_target_pairs={{0,4},{1,5},{2,6},{3,7},{4,0},{5,1},{6,2},{7,3},{8,12},{9,13},{10,... | collective-permute-start | bytes 208904 | tf_op jit(solution)/shard_map/ppermute | solution.py:797
  11.2 3.9 %collective-permute-start.5 = (f32[4,8,128]{2,1,0:T(8,128)S(1)}, f32[4,8,128]{2,1,0:T(8,128)S(1)}, u32[]{:S(2)}, u32[]{:S(2)}) collective-permute-start(f32[4,8,128]{2,1,0:T(8,128)S(1)} %get-tuple-element.62), channel_id=1, source_target_pairs={{0,12},{4,8},{8,4},{12,0},{16,28},{20,24},{24,20},{28,16},{1,13},{... | collective-permute-start | bytes 49160 | tf_op jit(solution)/shard_map/ppermute | solution.py:797
  12.0 4.1 %collective-permute-start.6 = (f32[4,8,128]{2,1,0:T(8,128)S(1)}, f32[4,8,128]{2,1,0:T(8,128)S(1)}, u32[]{:S(2)}, u32[]{:S(2)}) collective-permute-start(f32[4,8,128]{2,1,0:T(8,128)S(1)} %get-tuple-element.63), channel_id=1, source_target_pairs={{0,4},{4,0},{8,20},{12,16},{16,12},{20,8},{24,28},{28,24},{1,5},{5... | collective-permute-start | bytes 49160 | tf_op jit(solution)/shard_map/ppermute | solution.py:797
where the time goes:
time: 18.4 us; the launch traced here: 18.3 us
  starting transfers between devices  8.35 us (45%)
  Pallas kernels  6.31 us (34%)
  waiting for transfers between devices  2.94 us (16%)
  between operations  0.69 us (4%)
    ppermute x7, starting transfers between devices, swap(): return lax.ppermute(value, tuple(axes), pairs)  8.35 us
    pallas_call x6, Pallas kernels, call(): pl.pallas_call(kernel, out_shape=shapes, compiler_params=params, name=nam...  6.31 us
    ppermute x7, waiting for transfers between devices, swap(): return lax.ppermute(value, tuple(axes), pairs)  2.94 us
  transfers between devices with their start and end apart: 7, of which 3 were waited for; matrix products, arithmetic and copies ran while one was open for 0% of the time, Pallas kernels for 10%

commit v1 on v0

--- a/solution.py
+++ b/solution.py
@@ -456,6 +456,9 @@
 
 
 class Plane:
+    def across(self, shares, side, line):
+        return shares[side, line, pl.ds(8 + self.row, 8), :]
+
     def rim(self, shares, line, toward):
         if toward != (-1 if self.row < 0 else 1):
             return 0.0
@@ -474,6 +477,10 @@
 class Rim:
     def __init__(self, x, ext_y):
         self.x, self.ext_y = x, ext_y
+
+    def across(self, shares, side, line):
+        upper, lower = shares[side, line, pl.ds(8 + self.ext_y - 1, 8), :], shares[side, line, pl.ds(1, 8), :]
+        return jnp.where(lax.broadcasted_iota(jnp.int32, (8, LANES), 0) < 4, upper, lower)
 
     def rim(self, shares, line, toward):
         start = 1 if toward < 0 else 8 + self.ext_y - 1
@@ -509,7 +516,7 @@
         for j in range(19):
             value = after[j]
             if side is not None and VELOCITIES[j][0] == 2 * side - 1:
-                value = value + shares[side, pops(0, 2 * side - 1).index(j), pl.ds(8 + tile.row, 8), :]
+                value = value + tile.across(shares, side, pops(0, 2 * side - 1).index(j))
             if side is None and y_shares is not None and VELOCITIES[j][1]:
                 value = value + tile.rim(y_shares, pops(1, VELOCITIES[j][1]).index(j), VELOCITIES[j][1])
             if outside:
@@ -552,10 +559,43 @@
         z_first[tile, rows, :] = jnp.where(inside, moved, z_first[tile, rows, :])
 
 
+def z_step(z_first, z_second, starts):
+    lane = lane_ids()
+    loaded = []
+    for row in starts:
+
+        def both(low_tile, high_tile, group, cx, cy):
+            rows = pl.ds(8 + row + cy, 8)
+            low = pltpu.roll(z_first[low_tile, rows, :], (-GROUP * group - cx) % LANES, 1)
+            high = pltpu.roll(z_first[high_tile, rows, :], (LANES // 2 - GROUP * group - cx) % LANES, 1)
+            return jnp.where(lane < LANES // 2, low, high)
+
+        pulled = []
+        for j in range(19):
+            cx, cy, cz = VELOCITIES[j]
+            if cz == 0:
+                tile, group = Z_PLACE[("pop", j)]
+                pulled.append(both(BELOW + tile, ABOVE + tile, group, cx, cy))
+            elif cz == 1:
+                pulled.append(both(OWN_LOW, ABOVE + 2, Z_UP.index(j), cx, cy))
+            else:
+                pulled.append(both(BELOW + 2, OWN_HIGH, Z_DOWN.index(j), cx, cy))
+        places = [Z_PLACE[("field", k)] for k in range(5)]
+        loaded.append((pulled, [both(BELOW + tile, ABOVE + tile, group, 0, 0) for tile, group in places]))
+    done = [
+        collide(pulled, 1.0 / rho, rho, ux, uy, uz, kind > 1.5, Z_UP + Z_DOWN)[0]
+        for pulled, (rho, ux, uy, uz, kind) in loaded
+    ]
+    for row, (_, here), after in zip(starts, loaded, done):
+        for group in range(5):
+            value = jnp.where(lane < LANES // 2, after[Z_DOWN[group]], after[Z_UP[group]])
+            z_second[group, pl.ds(8 + row, 8), :] = jnp.where(here[KIND] > 0.5, value, 0.0)
+
+
 def side_kernel(slots, z_set, *rest):
     many_x, many_y = slots
     from_x, from_y = rest[4 : 4 + many_x], rest[4 + many_x : 4 + many_x + many_y]
-    first, fields, second, change, z_first, shares, y_shares = rest[-7:]
+    first, fields, second, change, z_first, z_second, shares, y_shares = rest[-8:]
     _, ext_y, _ = z_set.shape
     ext_x = change.shape[1] - 2
     inner = pl.ds(8, ext_y)
@@ -630,10 +670,10 @@
     for slot_x in range(many_x):
         on_side(parity_of("gx"), slot_x, functools.partial(place_x, slot_x))
 
-    rims = range(7, ext_y - 8, 8)
-    first_step(first, fields, second, change, [Plane(x, row) for x in (0, ext_x - 1) for row in rims], outside=False)
-    first_step(first, fields, second, change, [Plane(x, row) for x in (-1, ext_x) for row in rims], shares=shares)
-
+    starts = range(1, ext_y, 8)
+    first_step(first, fields, second, change, [Plane(x, row) for x in (0, ext_x - 1) for row in starts], outside=False)
+    first_step(first, fields, second, change, [Plane(x, row) for x in (-1, ext_x) for row in starts], shares=shares)
+    z_step(z_first, z_second, range(7, ext_y - 8, 8))
     many = 3 if (ext_x - 2) % 3 == 0 else 1
 
     @pl.loop(0, (ext_x - 2) // many)
@@ -644,9 +684,9 @@
 
 def last_kernel(slots, den, vel, mask, *rest):
     many_x, many_y = slots
-    from_xy = rest[7 : 7 + many_x * many_y]
-    out, sens, first, fields, second, change, z_first, shares, y_shares = rest[-13:-4]
-    z_second, held, held_sens, sems = rest[-4:]
+    from_xy = rest[8 : 8 + many_x * many_y]
+    out, sens, first, fields, second, change, z_first, z_second, shares, y_shares = rest[-13:-3]
+    held, held_sens, sems = rest[-3:]
     ext_x, ext_y, _ = mask.shape
     lane = lane_ids()
     every = slice(None)
@@ -669,39 +709,10 @@
             )
 
     for pair in ((-1, 0), (ext_x - 1, ext_x)):
-        tiles = [Plane(x, row) for x in pair for row in (-1, ext_y - 1)]
+        tiles = [Rim(x, ext_y) for x in pair]
         first_step(first, fields, second, change, tiles, shares=shares, y_shares=y_shares)
 
-    starts = [7 + 8 * part for part in range((ext_y + 2 + 7) // 8)]
-    loaded = []
-    for row in starts:
-
-        def both(low_tile, high_tile, group, cx, cy):
-            rows = pl.ds(row + cy, 8)
-            low = pltpu.roll(z_first[low_tile, rows, :], (-GROUP * group - cx) % LANES, 1)
-            high = pltpu.roll(z_first[high_tile, rows, :], (LANES // 2 - GROUP * group - cx) % LANES, 1)
-            return jnp.where(lane < LANES // 2, low, high)
-
-        pulled = []
-        for j in range(19):
-            cx, cy, cz = VELOCITIES[j]
-            if cz == 0:
-                tile, group = Z_PLACE[("pop", j)]
-                pulled.append(both(BELOW + tile, ABOVE + tile, group, cx, cy))
-            elif cz == 1:
-                pulled.append(both(OWN_LOW, ABOVE + 2, Z_UP.index(j), cx, cy))
-            else:
-                pulled.append(both(BELOW + 2, OWN_HIGH, Z_DOWN.index(j), cx, cy))
-        places = [Z_PLACE[("field", k)] for k in range(5)]
-        loaded.append((pulled, [both(BELOW + tile, ABOVE + tile, group, 0, 0) for tile, group in places]))
-    done = [
-        collide(pulled, 1.0 / rho, rho, ux, uy, uz, kind > 1.5, Z_UP + Z_DOWN)[0]
-        for pulled, (rho, ux, uy, uz, kind) in loaded
-    ]
-    for row, (_, here), after in zip(starts, loaded, done):
-        for group in range(5):
-            value = jnp.where(lane < LANES // 2, after[Z_DOWN[group]], after[Z_UP[group]])
-            z_second[group, pl.ds(row, 8), :] = jnp.where(here[KIND] > 0.5, value, 0.0)
+    z_step(z_first, z_second, (-1, ext_y - 1))
 
     def copies(x):
         return (
@@ -709,12 +720,8 @@
             pltpu.make_async_copy(held_sens.at[x], sens.at[x], sems.at[1, x]),
         )
 
-    many = 4 if ext_x % 4 == 0 else 1
-
-    @pl.loop(0, ext_x // many)
-    def _(group):
+    def second_step(planes):
         loaded = []
-        planes = [many * group + at for at in range(many)]
         for x, part in itertools.product(planes, range(ext_y // 8)):
             row = 8 + 8 * part
             pulled = []
@@ -743,6 +750,12 @@
         for x in planes:
             for copy in copies(x):
                 copy.start()
+
+    second_step(range(ext_x // 2))
+
+    @pl.loop(ext_x // 4, ext_x // 2)
+    def _(pair):
+        second_step([2 * pair, 2 * pair + 1])
 
     for x in range(ext_x):
         for copy in copies(x):
@@ -865,7 +878,7 @@
         functools.partial(side_kernel, (many_x, many_y)),
         "side_step",
         (z_set, *inout, *from_x, *from_y),
-        [array(*value.shape) for value in inout] + [array(Z_TILES, rows, LANES), array(2, 5, rows, LANES), array(5, ext_x, rows, LANES)],
+        [array(*value.shape) for value in inout] + [array(Z_TILES, rows, LANES), array(5, rows, LANES), array(2, 5, rows, LANES), array(5, ext_x, rows, LANES)],
         8,
         input_output_aliases={1 + at: at for at in range(4)},
         cost_estimate=pl.CostEstimate(flops=40_000_000, bytes_accessed=8_000_000, transcendentals=0),
@@ -876,10 +889,9 @@
         (den, vel, mask, *inout, *from_xy),
         [array(19, ext_x, ext_y, LANES), array(ext_x, ext_y, LANES)] + [array(*value.shape) for value in inout],
         8,
-        out_specs=[hbm] * 2 + [vmem] * 7,
-        input_output_aliases={3 + at: 2 + at for at in range(7)},
+        out_specs=[hbm] * 2 + [vmem] * 8,
+        input_output_aliases={3 + at: 2 + at for at in range(8)},
         scratch_shapes=[
-            pltpu.VMEM((5, rows, LANES), jnp.float32),
             pltpu.VMEM((19, ext_x, ext_y, LANES), jnp.float32),
             pltpu.VMEM((ext_x, ext_y, LANES), jnp.float32),
             pltpu.SemaphoreType.DMA((2, ext_x)),

time: 18.4 us -> 18.2 us (0.989)
  transfers between devices with their start and end apart: 7 -> 7, of which waited for: 3 -> 3; matrix products, arithmetic and copies ran while one was open for 0% -> 0% of each run, Pallas kernels for 10% -> 11%
where the time goes in v1:
time: 18.2 us; the launch traced here: 18.1 us
  starting transfers between devices  8.35 us (46%)
  Pallas kernels  6.26 us (34%)
  waiting for transfers between devices  2.78 us (15%)
  between operations  0.69 us (4%)
    ppermute x7, starting transfers between devices, swap(): return lax.ppermute(value, tuple(axes), pairs)  8.35 us
    pallas_call x6, Pallas kernels, call(): pl.pallas_call(kernel, out_shape=shapes, compiler_params=params, name=nam...  6.26 us
    ppermute x7, waiting for transfers between devices, swap(): return lax.ppermute(value, tuple(axes), pairs)  2.78 us
  transfers between devices with their start and end apart: 7, of which 3 were waited for; matrix products, arithmetic and copies ran while one was open for 0% of the time, Pallas kernels for 11%

profile of v1, /device:TPU:9, one launch (start us, length us, event | category | flops | bytes accessed | tf_op | source)
XLA Modules:
  0.0 18.1 jit_solution(14595911450350927886)
XLA Ops:
  0.6 1.9 %pack_z.1 = (f32[19,8,16,128]{3,2,1,0:T(8,128)S(1)}, f32[2,8,16,128]{3,2,1,0:T(8,128)S(1)}, f32[2,3,8,16,128]{4,3,2,1,0:T(8,128)S(1)}, s32[8,16,128]{2,1,0:T(8,1...) custom-call(f32[19,8,16,128]{3,2,1,0:T(8,128)} %adj_in.1, ...), custom_call_target="tpu_custom_call" | custom-call | tf_op jit(solution)/shard_map/pack_z/pallas_call | solution.py:781
  2.5 0.1 collective-permute-start
  2.6 2.6 %collective-permute-start.1 = (f32[3,16,128]{2,1,0:T(8,128)S(1)}, f32[3,16,128]{2,1,0:T(8,128)S(1)}, u32[]{:S(2)}, u32[]{:S(2)}) collective-permute-start(f32[3,16,128]{2,1,0:T(8,128)S(1)} %get-tuple-element.40), channel_id=1, source_target_pairs={{0,8},{1,2},{2,1},{3,11},{8,0},{9,10},{10,9},{11,3},{16,24},{17,18... | collective-permute-start | bytes 73736 | tf_op jit(solution)/shard_map/ppermute | solution.py:810
  5.2 0.4 %shift.1 = (f32[19,12,32,128]{3,2,1,0:T(8,128)S(1)}, f32[16,16,128]{2,1,0:T(8,128)S(1)}, f32[16,16,128]{2,1,0:T(8,128)S(1)}, f32[24,8,128]{2,1,0:T(8,128)S(1)}, ...) custom-call(f32[19,8,16,128]{3,2,1,0:T(8,128)S(1)} %get-tuple-element.41.adj, ...), custom_call_target="tpu_custom_call" | custom-call | flops 1000000 | bytes 2500000 | tf_op jit(solution)/shard_map/shift/pallas_call | solution.py:781
  5.5 0.0 collective-permute-done.rest_0_
  5.5 1.1 %collective-permute-done.1.rest_1_ = f32[3,16,128]{2,1,0:T(8,128)S(1)} collective-permute-done((f32[3,16,128]{2,1,0:T(8,128)S(1)}, f32[3,16,128]{2,1,0:T(8,128)S(1)}, u32[]{:S(2)}, u32[]{:S(2)}) %collective-permute-start.1) | collective-permute-done | bytes 24608 | tf_op jit(solution)/shard_map/ppermute | solution.py:810
  6.7 0.5 %pack_xy.1 = (f32[8,16,128]{2,1,0:T(8,128)S(1)}, f32[19,12,32,128]{3,2,1,0:T(8,128)S(1)}, f32[16,16,128]{2,1,0:T(8,128)S(1)}, f32[16,16,128]{2,1,0:T(8,128)S(1)}...) custom-call(f32[2,8,16,128]{3,2,1,0:T(8,128)S(1)} %get-tuple-element, ...), custom_call_target="tpu_custom_call", output_to_operand_aliasing={{1}: (6, {}), {2}: (7, {}), {3}: (8, {}), {4}: (9, {}), {5}... | custom-call | tf_op jit(solution)/shard_map/pack_xy/pallas_call | solution.py:781
  7.2 1.6 %collective-permute-start.2 = (f32[16,16,128]{2,1,0:T(8,128)S(1)}, f32[16,16,128]{2,1,0:T(8,128)S(1)}, u32[]{:S(2)}, u32[]{:S(2)}) collective-permute-start(f32[16,16,128]{2,1,0:T(8,128)S(1)} %get-tuple-element.53), channel_id=1, source_target_pairs={{0,8},{1,9},{2,10},{3,11},{8,0},{9,1},{10,2},{11,3},{16,24},{17,25... | collective-permute-start | bytes 393224 | tf_op jit(solution)/shard_map/ppermute | solution.py:810
  8.7 1.2 %collective-permute-start.3 = (f32[16,16,128]{2,1,0:T(8,128)S(1)}, f32[16,16,128]{2,1,0:T(8,128)S(1)}, u32[]{:S(2)}, u32[]{:S(2)}) collective-permute-start(f32[16,16,128]{2,1,0:T(8,128)S(1)} %get-tuple-element.54), channel_id=1, source_target_pairs={{0,24},{1,25},{2,3},{3,2},{8,16},{9,17},{10,18},{11,19},{16,8},{17... | collective-permute-start | bytes 393224 | tf_op jit(solution)/shard_map/ppermute | solution.py:810
  10.0 1.2 %collective-permute-start.4 = (f32[17,8,128]{2,1,0:T(8,128)S(1)}, f32[17,8,128]{2,1,0:T(8,128)S(1)}, u32[]{:S(2)}, u32[]{:S(2)}) collective-permute-start(f32[17,8,128]{2,1,0:T(8,128)S(1)} %get-tuple-element.55), channel_id=1, source_target_pairs={{0,4},{1,5},{2,6},{3,7},{4,0},{5,1},{6,2},{7,3},{8,12},{9,13},{10,... | collective-permute-start | bytes 208904 | tf_op jit(solution)/shard_map/ppermute | solution.py:810
  11.2 0.8 %collective-permute-start.5 = (f32[4,8,128]{2,1,0:T(8,128)S(1)}, f32[4,8,128]{2,1,0:T(8,128)S(1)}, u32[]{:S(2)}, u32[]{:S(2)}) collective-permute-start(f32[4,8,128]{2,1,0:T(8,128)S(1)} %get-tuple-element.64), channel_id=1, source_target_pairs={{0,12},{4,8},{8,4},{12,0},{16,28},{20,24},{24,20},{28,16},{1,13},{... | collective-permute-start | bytes 49160 | tf_op jit(solution)/shard_map/ppermute | solution.py:810
  12.0 0.8 %collective-permute-start.6 = (f32[4,8,128]{2,1,0:T(8,128)S(1)}, f32[4,8,128]{2,1,0:T(8,128)S(1)}, u32[]{:S(2)}, u32[]{:S(2)}) collective-permute-start(f32[4,8,128]{2,1,0:T(8,128)S(1)} %get-tuple-element.65), channel_id=1, source_target_pairs={{0,4},{4,0},{8,20},{12,16},{16,12},{20,8},{24,28},{28,24},{1,5},{5... | collective-permute-start | bytes 49160 | tf_op jit(solution)/shard_map/ppermute | solution.py:810
  12.9 0.5 %inner_step.1 = (f32[5,10,32,128]{3,2,1,0:T(8,128)S(1)}, f32[19,10,32,128]{3,2,1,0:T(8,128)S(1)}, f32[1,10,32,128]{3,2,1,0:T(8,128)S(1)}) custom-call(f32[2,8,16,128]{3,2,1,0:T(8,128)S(1)} %get-tuple-element.35.den, f32[2,3,8,16,128]{4,3,2,1,0:T(8,128)S(1)} %get-tuple-element.36.vel, s32[8,16,128]{2,1,0:T(8,128)S(1)} %get-tuple-element.37.mask, ...), custom_call_target="tpu_custom_call" | custom-call | flops 40000000 | bytes 8000000 | tf_op jit(solution)/shard_map/inner_step/pallas_call | solution.py:781
  13.4 0.0 collective-permute-done.4.rest_6_
  13.4 0.0 collective-permute-done.2.rest_4_
  13.4 0.8 %collective-permute-done.3.rest_5_ = f32[16,16,128]{2,1,0:T(8,128)S(1)} collective-permute-done((f32[16,16,128]{2,1,0:T(8,128)S(1)}, f32[16,16,128]{2,1,0:T(8,128)S(1)}, u32[]{:S(2)}, u32[]{:S(2)}) %collective-permute-start.3) | collective-permute-done | bytes 131104 | tf_op jit(solution)/shard_map/ppermute | solution.py:810
  14.2 1.1 %side_step.1 = (f32[19,12,32,128]{3,2,1,0:T(8,128)S(1)}, f32[5,10,32,128]{3,2,1,0:T(8,128)S(1)}, f32[19,10,32,128]{3,2,1,0:T(8,128)S(1)}, f32[1,10,32,128]{3,2,1...) custom-call(f32[8,16,128]{2,1,0:T(8,128)S(1)} %get-tuple-element.48., ...), custom_call_target="tpu_custom_call", output_to_operand_aliasing={{0}: (1, {}), {1}: (2, {}), {2}: (3, {}), {3}: (4, {})} | custom-call | flops 40000000 | bytes 8000000 | tf_op jit(solution)/shard_map/side_step/pallas_call | solution.py:781
  15.3 0.0 collective-permute-done.5.rest_8_
  15.3 0.8 %collective-permute-done.6.rest_9_ = f32[4,8,128]{2,1,0:T(8,128)S(1)} collective-permute-done((f32[4,8,128]{2,1,0:T(8,128)S(1)}, f32[4,8,128]{2,1,0:T(8,128)S(1)}, u32[]{:S(2)}, u32[]{:S(2)}) %collective-permute-start.6) | collective-permute-done | bytes 16416 | tf_op jit(solution)/shard_map/ppermute | solution.py:810
  16.1 2.0 %last_steps.1 = (f32[19,8,16,128]{3,2,1,0:T(8,128)}, f32[8,16,128]{2,1,0:T(8,128)}, f32[19,12,32,128]{3,2,1,0:T(8,128)S(1)}, f32[5,10,32,128]{3,2,1,0:T(8,128)S(...) custom-call(f32[2,8,16,128]{3,2,1,0:T(8,128)S(1)} %get-tuple-element, ...), custom_call_target="tpu_custom_call", output_to_operand_aliasing={{2}: (3, {}), {3}: (4, {}), {4}: (5, {}), {5}: (6, {}), {6}... | custom-call | tf_op jit(solution)/shard_map/last_steps/pallas_call | solution.py:781
Async XLA Ops:
  2.5 3.0 %collective-permute-start = (f32[3,16,128]{2,1,0:T(8,128)S(1)}, f32[3,16,128]{2,1,0:T(8,128)S(1)}, u32[]{:S(2)}, u32[]{:S(2)}) collective-permute-start(f32[3,16,128]{2,1,0:T(8,128)S(1)} %get-tuple-element.39), channel_id=1, source_target_pairs={{0,1},{1,0},{2,3},{3,2},{8,9},{9,8},{10,11},{11,10},{16,17},{17,16... | collective-permute-start | bytes 73736 | tf_op jit(solution)/shard_map/ppermute | solution.py:810
  2.6 4.1 %collective-permute-start.1 = (f32[3,16,128]{2,1,0:T(8,128)S(1)}, f32[3,16,128]{2,1,0:T(8,128)S(1)}, u32[]{:S(2)}, u32[]{:S(2)}) collective-permute-start(f32[3,16,128]{2,1,0:T(8,128)S(1)} %get-tuple-element.40), channel_id=1, source_target_pairs={{0,8},{1,2},{2,1},{3,11},{8,0},{9,10},{10,9},{11,3},{16,24},{17,18... | collective-permute-start | bytes 73736 | tf_op jit(solution)/shard_map/ppermute | solution.py:810
  7.2 6.2 %collective-permute-start.2 = (f32[16,16,128]{2,1,0:T(8,128)S(1)}, f32[16,16,128]{2,1,0:T(8,128)S(1)}, u32[]{:S(2)}, u32[]{:S(2)}) collective-permute-start(f32[16,16,128]{2,1,0:T(8,128)S(1)} %get-tuple-element.53), channel_id=1, source_target_pairs={{0,8},{1,9},{2,10},{3,11},{8,0},{9,1},{10,2},{11,3},{16,24},{17,25... | collective-permute-start | bytes 393224 | tf_op jit(solution)/shard_map/ppermute | solution.py:810
  8.7 5.5 %collective-permute-start.3 = (f32[16,16,128]{2,1,0:T(8,128)S(1)}, f32[16,16,128]{2,1,0:T(8,128)S(1)}, u32[]{:S(2)}, u32[]{:S(2)}) collective-permute-start(f32[16,16,128]{2,1,0:T(8,128)S(1)} %get-tuple-element.54), channel_id=1, source_target_pairs={{0,24},{1,25},{2,3},{3,2},{8,16},{9,17},{10,18},{11,19},{16,8},{17... | collective-permute-start | bytes 393224 | tf_op jit(solution)/shard_map/ppermute | solution.py:810
  10.0 3.5 %collective-permute-start.4 = (f32[17,8,128]{2,1,0:T(8,128)S(1)}, f32[17,8,128]{2,1,0:T(8,128)S(1)}, u32[]{:S(2)}, u32[]{:S(2)}) collective-permute-start(f32[17,8,128]{2,1,0:T(8,128)S(1)} %get-tuple-element.55), channel_id=1, source_target_pairs={{0,4},{1,5},{2,6},{3,7},{4,0},{5,1},{6,2},{7,3},{8,12},{9,13},{10,... | collective-permute-start | bytes 208904 | tf_op jit(solution)/shard_map/ppermute | solution.py:810
  11.2 4.1 %collective-permute-start.5 = (f32[4,8,128]{2,1,0:T(8,128)S(1)}, f32[4,8,128]{2,1,0:T(8,128)S(1)}, u32[]{:S(2)}, u32[]{:S(2)}) collective-permute-start(f32[4,8,128]{2,1,0:T(8,128)S(1)} %get-tuple-element.64), channel_id=1, source_target_pairs={{0,12},{4,8},{8,4},{12,0},{16,28},{20,24},{24,20},{28,16},{1,13},{... | collective-permute-start | bytes 49160 | tf_op jit(solution)/shard_map/ppermute | solution.py:810
  12.0 4.1 %collective-permute-start.6 = (f32[4,8,128]{2,1,0:T(8,128)S(1)}, f32[4,8,128]{2,1,0:T(8,128)S(1)}, u32[]{:S(2)}, u32[]{:S(2)}) collective-permute-start(f32[4,8,128]{2,1,0:T(8,128)S(1)} %get-tuple-element.65), channel_id=1, source_target_pairs={{0,4},{4,0},{8,20},{12,16},{16,12},{20,8},{24,28},{28,24},{1,5},{5... | collective-permute-start | bytes 49160 | tf_op jit(solution)/shard_map/ppermute | solution.py:810

commit v2 on v1

--- a/solution.py
+++ b/solution.py
@@ -592,10 +592,43 @@
             z_second[group, pl.ds(8 + row, 8), :] = jnp.where(here[KIND] > 0.5, value, 0.0)
 
 
-def side_kernel(slots, z_set, *rest):
+def second_step(refs, second, z_second, change, held, held_sens, planes):
+    den, vel, mask = refs
+    _, ext_y, _ = mask.shape
+    lane = lane_ids()
+    every = slice(None)
+    loaded = []
+    for x, part in itertools.product(planes, range(ext_y // 8)):
+        row = 8 + 8 * part
+        pulled = []
+        for j in range(19):
+            cx, cy, cz = VELOCITIES[j]
+            rows = pl.ds(row + cy, 8)
+            value = second[j, x + 1 + cx, rows, :]
+            if cz == 1:
+                edge = z_second[Z_UP.index(j), rows, :]
+                edge = pltpu.roll(edge, LANES // 2 - 3 - cx - x, 1)
+                value = jnp.where(lane == LANES - 1, edge, value)
+            elif cz == -1:
+                edge = z_second[Z_DOWN.index(j), rows, :]
+                edge = pltpu.roll(edge, LANES - 2 - cx - x, 1)
+                value = jnp.where(lane == 0, edge, value)
+            pulled.append(value)
+        at = (x, pl.ds(8 * part, 8), every)
+        rho = den[(0, *at)]
+        here = [1.0 / rho, rho, vel[(0, 0, *at)], vel[(0, 1, *at)], vel[(0, 2, *at)], mask[at] > 0]
+        loaded.append((at, pulled, here, change[0, x + 1, pl.ds(row, 8), :]))
+    done = [collide(pulled, *here, range(19)) for _, pulled, here, _ in loaded]
+    for (at, _, _, before), (after, gain) in zip(loaded, done):
+        for j in range(19):
+            held[(j, *at)] = after[j]
+        held_sens[at] = before + gain
+
+
+def side_kernel(slots, den, vel, mask, z_set, *rest):
     many_x, many_y = slots
     from_x, from_y = rest[4 : 4 + many_x], rest[4 + many_x : 4 + many_x + many_y]
-    first, fields, second, change, z_first, z_second, shares, y_shares = rest[-8:]
+    first, fields, second, change, z_first, z_second, shares, y_shares, held, held_sens = rest[-10:]
     _, ext_y, _ = z_set.shape
     ext_x = change.shape[1] - 2
     inner = pl.ds(8, ext_y)
@@ -681,16 +714,28 @@
         tiles = [Rim(many * group + at + 1, ext_y) for at in range(many)]
         first_step(first, fields, second, change, tiles, y_shares=y_shares)
 
+    z_step(z_first, z_second, (-1, ext_y - 1))
+    second_step((den, vel, mask), second, z_second, change, held, held_sens, range(2, ext_x - 2))
+
 
 def last_kernel(slots, den, vel, mask, *rest):
     many_x, many_y = slots
-    from_xy = rest[8 : 8 + many_x * many_y]
-    out, sens, first, fields, second, change, z_first, z_second, shares, y_shares = rest[-13:-3]
-    held, held_sens, sems = rest[-3:]
+    from_xy = rest[10 : 10 + many_x * many_y]
+    out, sens, first, fields, second, change, z_first, z_second, shares, y_shares, held, held_sens, sems = rest[-13:]
     ext_x, ext_y, _ = mask.shape
     lane = lane_ids()
     every = slice(None)
     px, py = parity_of("gx"), parity_of("gy")
+
+    def copies(x):
+        return (
+            pltpu.make_async_copy(held.at[:, x], out.at[:, x], sems.at[0, x]),
+            pltpu.make_async_copy(held_sens.at[x], sens.at[x], sems.at[1, x]),
+        )
+
+    for x in range(2, ext_x - 2):
+        for copy in copies(x):
+            copy.start()
 
     def place_xy(slot_x, slot_y, side_x, side_y):
         packet = from_xy[many_x * slot_y + slot_x]
@@ -714,48 +759,12 @@
 
     z_step(z_first, z_second, (-1, ext_y - 1))
 
-    def copies(x):
-        return (
-            pltpu.make_async_copy(held.at[:, x], out.at[:, x], sems.at[0, x]),
-            pltpu.make_async_copy(held_sens.at[x], sens.at[x], sems.at[1, x]),
-        )
-
-    def second_step(planes):
-        loaded = []
-        for x, part in itertools.product(planes, range(ext_y // 8)):
-            row = 8 + 8 * part
-            pulled = []
-            for j in range(19):
-                cx, cy, cz = VELOCITIES[j]
-                rows = pl.ds(row + cy, 8)
-                value = second[j, x + 1 + cx, rows, :]
-                if cz == 1:
-                    edge = z_second[Z_UP.index(j), rows, :]
-                    edge = pltpu.roll(edge, LANES // 2 - 3 - cx - x, 1)
-                    value = jnp.where(lane == LANES - 1, edge, value)
-                elif cz == -1:
-                    edge = z_second[Z_DOWN.index(j), rows, :]
-                    edge = pltpu.roll(edge, LANES - 2 - cx - x, 1)
-                    value = jnp.where(lane == 0, edge, value)
-                pulled.append(value)
-            at = (x, pl.ds(8 * part, 8), every)
-            rho = den[(0, *at)]
-            here = [1.0 / rho, rho, vel[(0, 0, *at)], vel[(0, 1, *at)], vel[(0, 2, *at)], mask[at] > 0]
-            loaded.append((at, pulled, here, change[0, x + 1, pl.ds(row, 8), :]))
-        done = [collide(pulled, *here, range(19)) for _, pulled, here, _ in loaded]
-        for (at, _, _, before), (after, gain) in zip(loaded, done):
-            for j in range(19):
-                held[(j, *at)] = after[j]
-            held_sens[at] = before + gain
-        for x in planes:
+    planes = [0, 1, ext_x - 2, ext_x - 1]
+    for pair in (planes[:2], planes[2:]):
+        second_step((den, vel, mask), second, z_second, change, held, held_sens, pair)
+        for x in pair:
             for copy in copies(x):
                 copy.start()
-
-    second_step(range(ext_x // 2))
-
-    @pl.loop(ext_x // 4, ext_x // 2)
-    def _(pair):
-        second_step([2 * pair, 2 * pair + 1])
 
     for x in range(ext_x):
         for copy in copies(x):
@@ -877,10 +886,11 @@
     inout = call(
         functools.partial(side_kernel, (many_x, many_y)),
         "side_step",
-        (z_set, *inout, *from_x, *from_y),
-        [array(*value.shape) for value in inout] + [array(Z_TILES, rows, LANES), array(5, rows, LANES), array(2, 5, rows, LANES), array(5, ext_x, rows, LANES)],
+        (den, vel, mask, z_set, *inout, *from_x, *from_y),
+        [array(*value.shape) for value in inout] + [array(Z_TILES, rows, LANES), array(5, rows, LANES), array(2, 5, rows, LANES), array(5, ext_x, rows, LANES)]
+        + [array(19, ext_x, ext_y, LANES), array(ext_x, ext_y, LANES)],
         8,
-        input_output_aliases={1 + at: at for at in range(4)},
+        input_output_aliases={4 + at: at for at in range(4)},
         cost_estimate=pl.CostEstimate(flops=40_000_000, bytes_accessed=8_000_000, transcendentals=0),
     )
     return call(
@@ -889,13 +899,9 @@
         (den, vel, mask, *inout, *from_xy),
         [array(19, ext_x, ext_y, LANES), array(ext_x, ext_y, LANES)] + [array(*value.shape) for value in inout],
         8,
-        out_specs=[hbm] * 2 + [vmem] * 8,
-        input_output_aliases={3 + at: 2 + at for at in range(8)},
-        scratch_shapes=[
-            pltpu.VMEM((19, ext_x, ext_y, LANES), jnp.float32),
-            pltpu.VMEM((ext_x, ext_y, LANES), jnp.float32),
-            pltpu.SemaphoreType.DMA((2, ext_x)),
-        ],
+        out_specs=[hbm] * 2 + [vmem] * 10,
+        input_output_aliases={3 + at: 2 + at for at in range(10)},
+        scratch_shapes=[pltpu.SemaphoreType.DMA((2, ext_x))],
     )[:2]
 
 

time: 18.2 us -> 17.9 us (0.984)
  waiting for transfers between devices: 2.78 us -> 2.41 us
    ppermute x7, waiting for transfers between devices: 2.78 us -> 2.41 us  [swap(): return lax.ppermute(value, tuple(axes), pairs)]
  transfers between devices with their start and end apart: 7 -> 7, of which waited for: 3 -> 3; matrix products, arithmetic and copies ran while one was open for 0% -> 0% of each run, Pallas kernels for 11% -> 13%
where the time goes in v2:
time: 17.9 us; the launch traced here: 17.8 us
  starting transfers between devices  8.35 us (47%)
  Pallas kernels  6.31 us (35%)
  waiting for transfers between devices  2.41 us (13%)
  between operations  0.69 us (4%)
    ppermute x7, starting transfers between devices, swap(): return lax.ppermute(value, tuple(axes), pairs)  8.35 us
    pallas_call x6, Pallas kernels, call(): pl.pallas_call(kernel, out_shape=shapes, compiler_params=params, name=nam...  6.31 us
    ppermute x7, waiting for transfers between devices, swap(): return lax.ppermute(value, tuple(axes), pairs)  2.41 us
  transfers between devices with their start and end apart: 7, of which 3 were waited for; matrix products, arithmetic and copies ran while one was open for 0% of the time, Pallas kernels for 13%

profile of v2, /device:TPU:9, one launch (start us, length us, event | category | flops | bytes accessed | tf_op | source)
XLA Modules:
  0.0 17.8 jit_solution(10999946985553207874)
XLA Ops:
  0.6 1.9 %pack_z.1 = (f32[19,8,16,128]{3,2,1,0:T(8,128)S(1)}, f32[2,8,16,128]{3,2,1,0:T(8,128)S(1)}, f32[2,3,8,16,128]{4,3,2,1,0:T(8,128)S(1)}, s32[8,16,128]{2,1,0:T(8,1...) custom-call(f32[19,8,16,128]{3,2,1,0:T(8,128)} %adj_in.1, ...), custom_call_target="tpu_custom_call" | custom-call | tf_op jit(solution)/shard_map/pack_z/pallas_call | solution.py:790
  2.5 0.1 collective-permute-start
  2.6 2.6 %collective-permute-start.1 = (f32[3,16,128]{2,1,0:T(8,128)S(1)}, f32[3,16,128]{2,1,0:T(8,128)S(1)}, u32[]{:S(2)}, u32[]{:S(2)}) collective-permute-start(f32[3,16,128]{2,1,0:T(8,128)S(1)} %get-tuple-element.42), channel_id=1, source_target_pairs={{0,8},{1,2},{2,1},{3,11},{8,0},{9,10},{10,9},{11,3},{16,24},{17,18... | collective-permute-start | bytes 73736 | tf_op jit(solution)/shard_map/ppermute | solution.py:819
  5.2 0.4 %shift.1 = (f32[19,12,32,128]{3,2,1,0:T(8,128)S(1)}, f32[16,16,128]{2,1,0:T(8,128)S(1)}, f32[16,16,128]{2,1,0:T(8,128)S(1)}, f32[24,8,128]{2,1,0:T(8,128)S(1)}, ...) custom-call(f32[19,8,16,128]{3,2,1,0:T(8,128)S(1)} %get-tuple-element.43.adj, ...), custom_call_target="tpu_custom_call" | custom-call | flops 1000000 | bytes 2500000 | tf_op jit(solution)/shard_map/shift/pallas_call | solution.py:790
  5.5 0.0 collective-permute-done.rest_0_
  5.5 1.1 %collective-permute-done.1.rest_1_ = f32[3,16,128]{2,1,0:T(8,128)S(1)} collective-permute-done((f32[3,16,128]{2,1,0:T(8,128)S(1)}, f32[3,16,128]{2,1,0:T(8,128)S(1)}, u32[]{:S(2)}, u32[]{:S(2)}) %collective-permute-start.1) | collective-permute-done | bytes 24608 | tf_op jit(solution)/shard_map/ppermute | solution.py:819
  6.7 0.5 %pack_xy.1 = (f32[8,16,128]{2,1,0:T(8,128)S(1)}, f32[19,12,32,128]{3,2,1,0:T(8,128)S(1)}, f32[16,16,128]{2,1,0:T(8,128)S(1)}, f32[16,16,128]{2,1,0:T(8,128)S(1)}...) custom-call(f32[2,8,16,128]{3,2,1,0:T(8,128)S(1)} %get-tuple-element, ...), custom_call_target="tpu_custom_call", output_to_operand_aliasing={{1}: (6, {}), {2}: (7, {}), {3}: (8, {}), {4}: (9, {}), {5}... | custom-call | tf_op jit(solution)/shard_map/pack_xy/pallas_call | solution.py:790
  7.2 1.6 %collective-permute-start.2 = (f32[16,16,128]{2,1,0:T(8,128)S(1)}, f32[16,16,128]{2,1,0:T(8,128)S(1)}, u32[]{:S(2)}, u32[]{:S(2)}) collective-permute-start(f32[16,16,128]{2,1,0:T(8,128)S(1)} %get-tuple-element.55), channel_id=1, source_target_pairs={{0,8},{1,9},{2,10},{3,11},{8,0},{9,1},{10,2},{11,3},{16,24},{17,25... | collective-permute-start | bytes 393224 | tf_op jit(solution)/shard_map/ppermute | solution.py:819
  8.7 1.2 %collective-permute-start.3 = (f32[16,16,128]{2,1,0:T(8,128)S(1)}, f32[16,16,128]{2,1,0:T(8,128)S(1)}, u32[]{:S(2)}, u32[]{:S(2)}) collective-permute-start(f32[16,16,128]{2,1,0:T(8,128)S(1)} %get-tuple-element.56), channel_id=1, source_target_pairs={{0,24},{1,25},{2,3},{3,2},{8,16},{9,17},{10,18},{11,19},{16,8},{17... | collective-permute-start | bytes 393224 | tf_op jit(solution)/shard_map/ppermute | solution.py:819
  9.9 1.2 %collective-permute-start.4 = (f32[17,8,128]{2,1,0:T(8,128)S(1)}, f32[17,8,128]{2,1,0:T(8,128)S(1)}, u32[]{:S(2)}, u32[]{:S(2)}) collective-permute-start(f32[17,8,128]{2,1,0:T(8,128)S(1)} %get-tuple-element.57), channel_id=1, source_target_pairs={{0,4},{1,5},{2,6},{3,7},{4,0},{5,1},{6,2},{7,3},{8,12},{9,13},{10,... | collective-permute-start | bytes 208904 | tf_op jit(solution)/shard_map/ppermute | solution.py:819
  11.2 0.8 %collective-permute-start.5 = (f32[4,8,128]{2,1,0:T(8,128)S(1)}, f32[4,8,128]{2,1,0:T(8,128)S(1)}, u32[]{:S(2)}, u32[]{:S(2)}) collective-permute-start(f32[4,8,128]{2,1,0:T(8,128)S(1)} %get-tuple-element.68), channel_id=1, source_target_pairs={{0,12},{4,8},{8,4},{12,0},{16,28},{20,24},{24,20},{28,16},{1,13},{... | collective-permute-start | bytes 49160 | tf_op jit(solution)/shard_map/ppermute | solution.py:819
  12.0 0.8 %collective-permute-start.6 = (f32[4,8,128]{2,1,0:T(8,128)S(1)}, f32[4,8,128]{2,1,0:T(8,128)S(1)}, u32[]{:S(2)}, u32[]{:S(2)}) collective-permute-start(f32[4,8,128]{2,1,0:T(8,128)S(1)} %get-tuple-element.69), channel_id=1, source_target_pairs={{0,4},{4,0},{8,20},{12,16},{16,12},{20,8},{24,28},{28,24},{1,5},{5... | collective-permute-start | bytes 49160 | tf_op jit(solution)/shard_map/ppermute | solution.py:819
  12.9 0.5 %inner_step.1 = (f32[5,10,32,128]{3,2,1,0:T(8,128)S(1)}, f32[19,10,32,128]{3,2,1,0:T(8,128)S(1)}, f32[1,10,32,128]{3,2,1,0:T(8,128)S(1)}) custom-call(f32[2,8,16,128]{3,2,1,0:T(8,128)S(1)} %get-tuple-element.37.den, f32[2,3,8,16,128]{4,3,2,1,0:T(8,128)S(1)} %get-tuple-element.38.vel, s32[8,16,128]{2,1,0:T(8,128)S(1)} %get-tuple-element.39.mask, ...), custom_call_target="tpu_custom_call" | custom-call | flops 40000000 | bytes 8000000 | tf_op jit(solution)/shard_map/inner_step/pallas_call | solution.py:790
  13.4 0.0 collective-permute-done.4.rest_6_
  13.4 0.0 collective-permute-done.2.rest_4_
  13.4 0.8 %collective-permute-done.3.rest_5_ = f32[16,16,128]{2,1,0:T(8,128)S(1)} collective-permute-done((f32[16,16,128]{2,1,0:T(8,128)S(1)}, f32[16,16,128]{2,1,0:T(8,128)S(1)}, u32[]{:S(2)}, u32[]{:S(2)}) %collective-permute-start.3) | collective-permute-done | bytes 131104 | tf_op jit(solution)/shard_map/ppermute | solution.py:819
  14.2 1.4 %side_step.1 = (f32[19,12,32,128]{3,2,1,0:T(8,128)S(1)}, f32[5,10,32,128]{3,2,1,0:T(8,128)S(1)}, f32[19,10,32,128]{3,2,1,0:T(8,128)S(1)}, f32[1,10,32,128]{3,2,1...) custom-call(f32[2,8,16,128]{3,2,1,0:T(8,128)S(1)} %get-tuple-element, ...), custom_call_target="tpu_custom_call", output_to_operand_aliasing={{0}: (4, {}), {1}: (5, {}), {2}: (6, {}), {3}: (7, {})} | custom-call | flops 40000000 | bytes 8000000 | tf_op jit(solution)/shard_map/side_step/pallas_call | solution.py:790
  15.7 0.0 collective-permute-done.5.rest_10_
  15.7 0.4 %collective-permute-done.6.rest_11_ = f32[4,8,128]{2,1,0:T(8,128)S(1)} collective-permute-done((f32[4,8,128]{2,1,0:T(8,128)S(1)}, f32[4,8,128]{2,1,0:T(8,128)S(1)}, u32[]{:S(2)}, u32[]{:S(2)}) %collective-permute-start.6) | collective-permute-done | bytes 16416 | tf_op jit(solution)/shard_map/ppermute | solution.py:819
  16.1 1.7 %last_steps.1 = (f32[19,8,16,128]{3,2,1,0:T(8,128)}, f32[8,16,128]{2,1,0:T(8,128)}, f32[19,12,32,128]{3,2,1,0:T(8,128)S(1)}, f32[5,10,32,128]{3,2,1,0:T(8,128)S(...) custom-call(f32[2,8,16,128]{3,2,1,0:T(8,128)S(1)} %get-tuple-element, ...), custom_call_target="tpu_custom_call", output_to_operand_aliasing={{2}: (3, {}), {3}: (4, {}), {4}: (5, {}), {5}: (6, {}), {6}... | custom-call | tf_op jit(solution)/shard_map/last_steps/pallas_call | solution.py:790
Async XLA Ops:
  2.5 3.0 %collective-permute-start = (f32[3,16,128]{2,1,0:T(8,128)S(1)}, f32[3,16,128]{2,1,0:T(8,128)S(1)}, u32[]{:S(2)}, u32[]{:S(2)}) collective-permute-start(f32[3,16,128]{2,1,0:T(8,128)S(1)} %get-tuple-element.41), channel_id=1, source_target_pairs={{0,1},{1,0},{2,3},{3,2},{8,9},{9,8},{10,11},{11,10},{16,17},{17,16... | collective-permute-start | bytes 73736 | tf_op jit(solution)/shard_map/ppermute | solution.py:819
  2.6 4.1 %collective-permute-start.1 = (f32[3,16,128]{2,1,0:T(8,128)S(1)}, f32[3,16,128]{2,1,0:T(8,128)S(1)}, u32[]{:S(2)}, u32[]{:S(2)}) collective-permute-start(f32[3,16,128]{2,1,0:T(8,128)S(1)} %get-tuple-element.42), channel_id=1, source_target_pairs={{0,8},{1,2},{2,1},{3,11},{8,0},{9,10},{10,9},{11,3},{16,24},{17,18... | collective-permute-start | bytes 73736 | tf_op jit(solution)/shard_map/ppermute | solution.py:819
  7.2 6.2 %collective-permute-start.2 = (f32[16,16,128]{2,1,0:T(8,128)S(1)}, f32[16,16,128]{2,1,0:T(8,128)S(1)}, u32[]{:S(2)}, u32[]{:S(2)}) collective-permute-start(f32[16,16,128]{2,1,0:T(8,128)S(1)} %get-tuple-element.55), channel_id=1, source_target_pairs={{0,8},{1,9},{2,10},{3,11},{8,0},{9,1},{10,2},{11,3},{16,24},{17,25... | collective-permute-start | bytes 393224 | tf_op jit(solution)/shard_map/ppermute | solution.py:819
  8.7 5.5 %collective-permute-start.3 = (f32[16,16,128]{2,1,0:T(8,128)S(1)}, f32[16,16,128]{2,1,0:T(8,128)S(1)}, u32[]{:S(2)}, u32[]{:S(2)}) collective-permute-start(f32[16,16,128]{2,1,0:T(8,128)S(1)} %get-tuple-element.56), channel_id=1, source_target_pairs={{0,24},{1,25},{2,3},{3,2},{8,16},{9,17},{10,18},{11,19},{16,8},{17... | collective-permute-start | bytes 393224 | tf_op jit(solution)/shard_map/ppermute | solution.py:819
  9.9 3.5 %collective-permute-start.4 = (f32[17,8,128]{2,1,0:T(8,128)S(1)}, f32[17,8,128]{2,1,0:T(8,128)S(1)}, u32[]{:S(2)}, u32[]{:S(2)}) collective-permute-start(f32[17,8,128]{2,1,0:T(8,128)S(1)} %get-tuple-element.57), channel_id=1, source_target_pairs={{0,4},{1,5},{2,6},{3,7},{4,0},{5,1},{6,2},{7,3},{8,12},{9,13},{10,... | collective-permute-start | bytes 208904 | tf_op jit(solution)/shard_map/ppermute | solution.py:819
  11.2 4.5 %collective-permute-start.5 = (f32[4,8,128]{2,1,0:T(8,128)S(1)}, f32[4,8,128]{2,1,0:T(8,128)S(1)}, u32[]{:S(2)}, u32[]{:S(2)}) collective-permute-start(f32[4,8,128]{2,1,0:T(8,128)S(1)} %get-tuple-element.68), channel_id=1, source_target_pairs={{0,12},{4,8},{8,4},{12,0},{16,28},{20,24},{24,20},{28,16},{1,13},{... | collective-permute-start | bytes 49160 | tf_op jit(solution)/shard_map/ppermute | solution.py:819
  12.0 4.1 %collective-permute-start.6 = (f32[4,8,128]{2,1,0:T(8,128)S(1)}, f32[4,8,128]{2,1,0:T(8,128)S(1)}, u32[]{:S(2)}, u32[]{:S(2)}) collective-permute-start(f32[4,8,128]{2,1,0:T(8,128)S(1)} %get-tuple-element.69), channel_id=1, source_target_pairs={{0,4},{4,0},{8,20},{12,16},{16,12},{20,8},{24,28},{28,24},{1,5},{5... | collective-permute-start | bytes 49160 | tf_op jit(solution)/shard_map/ppermute | solution.py:819

commit v3 on v2

--- a/solution.py
+++ b/solution.py
@@ -191,9 +191,10 @@
         near[1, rows, :] = high[1]
         for slot in range(slots):
             there = has_partner("gz", slot)
-            for tile in range(3):
-                value = jnp.where(parity == slot, high[tile], low[tile])
-                packets[slot][tile, rows, :] = jnp.where(there, value, 0.0)
+            sent = [jnp.where(there, jnp.where(parity == slot, up, down), 0.0) for up, down in zip(high, low)]
+            mine = (lane + (GROUP - 2)) % GROUP < GROUP // 2
+            packets[slot][0, rows, :] = jnp.where(mine, sent[0], pltpu.roll(sent[1], GROUP // 2, 1))
+            packets[slot][1, rows, :] = sent[2]
 
 
 def pack_lines(refs, first, packets, many_x, many_y, wanted, shares):
@@ -292,9 +293,15 @@
 
     z_set[OWN_LOW] = near[0]
     z_set[OWN_HIGH] = near[1]
+
+    def taken(slot, tile):
+        if tile == 1:
+            return pltpu.roll(from_z[slot][0], LANES - GROUP // 2, 1)
+        return from_z[slot][tile // 2]
+
     for tile in range(3):
-        even = from_z[0][tile]
-        odd = from_z[1][tile] if many_z > 1 else jnp.zeros_like(even)
+        even = taken(0, tile)
+        odd = taken(1, tile) if many_z > 1 else jnp.zeros_like(even)
         z_set[ABOVE + tile] = jnp.where(pz == 0, even, odd)
         z_set[BELOW + tile] = jnp.where(pz == 0, odd, even)
 
@@ -824,7 +831,7 @@
             functools.partial(pack_z_kernel, many_z),
             "pack_z",
             [pltpu.with_memory_space_constraint(value, pltpu.HBM) for value in inputs],
-            loaded + [array(2, ext_y, LANES)] + [array(3, ext_y, LANES)] * many_z,
+            loaded + [array(2, ext_y, LANES)] + [array(2, ext_y, LANES)] * many_z,
             8,
             in_specs=[hbm] * 4,
             scratch_shapes=[pltpu.SemaphoreType.DMA((7,))],

time: 17.9 us -> 17.9 us (level)
  no operation moved by 1% of the time
where the time goes in v3:
time: 17.9 us; the launch traced here: 17.8 us
  starting transfers between devices  8.35 us (47%)
  Pallas kernels  6.39 us (36%)
  waiting for transfers between devices  2.32 us (13%)
  between operations  0.69 us (4%)
    ppermute x7, starting transfers between devices, swap(): return lax.ppermute(value, tuple(axes), pairs)  8.35 us
    pallas_call x6, Pallas kernels, call(): pl.pallas_call(kernel, out_shape=shapes, compiler_params=params, name=nam...  6.39 us
    ppermute x7, waiting for transfers between devices, swap(): return lax.ppermute(value, tuple(axes), pairs)  2.32 us
  transfers between devices with their start and end apart: 7, of which 3 were waited for; matrix products, arithmetic and copies ran while one was open for 0% of the time, Pallas kernels for 13%

profile of v3, /device:TPU:9, one launch (start us, length us, event | category | flops | bytes accessed | tf_op | source)
XLA Modules:
  0.0 17.8 jit_solution(10184134743842739849)
XLA Ops:
  0.6 1.9 %pack_z.1 = (f32[19,8,16,128]{3,2,1,0:T(8,128)S(1)}, f32[2,8,16,128]{3,2,1,0:T(8,128)S(1)}, f32[2,3,8,16,128]{4,3,2,1,0:T(8,128)S(1)}, s32[8,16,128]{2,1,0:T(8,1...) custom-call(f32[19,8,16,128]{3,2,1,0:T(8,128)} %adj_in.1, ...), custom_call_target="tpu_custom_call" | custom-call | tf_op jit(solution)/shard_map/pack_z/pallas_call | solution.py:797
  2.5 0.1 collective-permute-start
  2.6 2.6 %collective-permute-start.1 = (f32[2,16,128]{2,1,0:T(8,128)S(1)}, f32[2,16,128]{2,1,0:T(8,128)S(1)}, u32[]{:S(2)}, u32[]{:S(2)}) collective-permute-start(f32[2,16,128]{2,1,0:T(8,128)S(1)} %get-tuple-element.42), channel_id=1, source_target_pairs={{0,8},{1,2},{2,1},{3,11},{8,0},{9,10},{10,9},{11,3},{16,24},{17,18... | collective-permute-start | bytes 49160 | tf_op jit(solution)/shard_map/ppermute | solution.py:826
  5.2 0.4 %shift.1 = (f32[19,12,32,128]{3,2,1,0:T(8,128)S(1)}, f32[16,16,128]{2,1,0:T(8,128)S(1)}, f32[16,16,128]{2,1,0:T(8,128)S(1)}, f32[24,8,128]{2,1,0:T(8,128)S(1)}, ...) custom-call(f32[19,8,16,128]{3,2,1,0:T(8,128)S(1)} %get-tuple-element.43.adj, ...), custom_call_target="tpu_custom_call" | custom-call | flops 1000000 | bytes 2500000 | tf_op jit(solution)/shard_map/shift/pallas_call | solution.py:797
  5.6 0.0 collective-permute-done.rest_0_
  5.6 1.0 %collective-permute-done.1.rest_1_ = f32[2,16,128]{2,1,0:T(8,128)S(1)} collective-permute-done((f32[2,16,128]{2,1,0:T(8,128)S(1)}, f32[2,16,128]{2,1,0:T(8,128)S(1)}, u32[]{:S(2)}, u32[]{:S(2)}) %collective-permute-start.1) | collective-permute-done | bytes 16416 | tf_op jit(solution)/shard_map/ppermute | solution.py:826
  6.6 0.6 %pack_xy.1 = (f32[8,16,128]{2,1,0:T(8,128)S(1)}, f32[19,12,32,128]{3,2,1,0:T(8,128)S(1)}, f32[16,16,128]{2,1,0:T(8,128)S(1)}, f32[16,16,128]{2,1,0:T(8,128)S(1)}...) custom-call(f32[2,8,16,128]{3,2,1,0:T(8,128)S(1)} %get-tuple-element, ...), custom_call_target="tpu_custom_call", output_to_operand_aliasing={{1}: (6, {}), {2}: (7, {}), {3}: (8, {}), {4}: (9, {}), {5}... | custom-call | tf_op jit(solution)/shard_map/pack_xy/pallas_call | solution.py:797
  7.2 1.6 %collective-permute-start.2 = (f32[16,16,128]{2,1,0:T(8,128)S(1)}, f32[16,16,128]{2,1,0:T(8,128)S(1)}, u32[]{:S(2)}, u32[]{:S(2)}) collective-permute-start(f32[16,16,128]{2,1,0:T(8,128)S(1)} %get-tuple-element.55), channel_id=1, source_target_pairs={{0,8},{1,9},{2,10},{3,11},{8,0},{9,1},{10,2},{11,3},{16,24},{17,25... | collective-permute-start | bytes 393224 | tf_op jit(solution)/shard_map/ppermute | solution.py:826
  8.7 1.2 %collective-permute-start.3 = (f32[16,16,128]{2,1,0:T(8,128)S(1)}, f32[16,16,128]{2,1,0:T(8,128)S(1)}, u32[]{:S(2)}, u32[]{:S(2)}) collective-permute-start(f32[16,16,128]{2,1,0:T(8,128)S(1)} %get-tuple-element.56), channel_id=1, source_target_pairs={{0,24},{1,25},{2,3},{3,2},{8,16},{9,17},{10,18},{11,19},{16,8},{17... | collective-permute-start | bytes 393224 | tf_op jit(solution)/shard_map/ppermute | solution.py:826
  9.9 1.2 %collective-permute-start.4 = (f32[17,8,128]{2,1,0:T(8,128)S(1)}, f32[17,8,128]{2,1,0:T(8,128)S(1)}, u32[]{:S(2)}, u32[]{:S(2)}) collective-permute-start(f32[17,8,128]{2,1,0:T(8,128)S(1)} %get-tuple-element.57), channel_id=1, source_target_pairs={{0,4},{1,5},{2,6},{3,7},{4,0},{5,1},{6,2},{7,3},{8,12},{9,13},{10,... | collective-permute-start | bytes 208904 | tf_op jit(solution)/shard_map/ppermute | solution.py:826
  11.2 0.8 %collective-permute-start.5 = (f32[4,8,128]{2,1,0:T(8,128)S(1)}, f32[4,8,128]{2,1,0:T(8,128)S(1)}, u32[]{:S(2)}, u32[]{:S(2)}) collective-permute-start(f32[4,8,128]{2,1,0:T(8,128)S(1)} %get-tuple-element.68), channel_id=1, source_target_pairs={{0,12},{4,8},{8,4},{12,0},{16,28},{20,24},{24,20},{28,16},{1,13},{... | collective-permute-start | bytes 49160 | tf_op jit(solution)/shard_map/ppermute | solution.py:826
  12.0 0.8 %collective-permute-start.6 = (f32[4,8,128]{2,1,0:T(8,128)S(1)}, f32[4,8,128]{2,1,0:T(8,128)S(1)}, u32[]{:S(2)}, u32[]{:S(2)}) collective-permute-start(f32[4,8,128]{2,1,0:T(8,128)S(1)} %get-tuple-element.69), channel_id=1, source_target_pairs={{0,4},{4,0},{8,20},{12,16},{16,12},{20,8},{24,28},{28,24},{1,5},{5... | collective-permute-start | bytes 49160 | tf_op jit(solution)/shard_map/ppermute | solution.py:826
  12.9 0.5 %inner_step.1 = (f32[5,10,32,128]{3,2,1,0:T(8,128)S(1)}, f32[19,10,32,128]{3,2,1,0:T(8,128)S(1)}, f32[1,10,32,128]{3,2,1,0:T(8,128)S(1)}) custom-call(f32[2,8,16,128]{3,2,1,0:T(8,128)S(1)} %get-tuple-element.37.den, f32[2,3,8,16,128]{4,3,2,1,0:T(8,128)S(1)} %get-tuple-element.38.vel, s32[8,16,128]{2,1,0:T(8,128)S(1)} %get-tuple-element.39.mask, ...), custom_call_target="tpu_custom_call" | custom-call | flops 40000000 | bytes 8000000 | tf_op jit(solution)/shard_map/inner_step/pallas_call | solution.py:797
  13.4 0.0 collective-permute-done.4.rest_6_
  13.4 0.0 collective-permute-done.2.rest_4_
  13.4 0.8 %collective-permute-done.3.rest_5_ = f32[16,16,128]{2,1,0:T(8,128)S(1)} collective-permute-done((f32[16,16,128]{2,1,0:T(8,128)S(1)}, f32[16,16,128]{2,1,0:T(8,128)S(1)}, u32[]{:S(2)}, u32[]{:S(2)}) %collective-permute-start.3) | collective-permute-done | bytes 131104 | tf_op jit(solution)/shard_map/ppermute | solution.py:826
  14.2 1.4 %side_step.1 = (f32[19,12,32,128]{3,2,1,0:T(8,128)S(1)}, f32[5,10,32,128]{3,2,1,0:T(8,128)S(1)}, f32[19,10,32,128]{3,2,1,0:T(8,128)S(1)}, f32[1,10,32,128]{3,2,1...) custom-call(f32[2,8,16,128]{3,2,1,0:T(8,128)S(1)} %get-tuple-element, ...), custom_call_target="tpu_custom_call", output_to_operand_aliasing={{0}: (4, {}), {1}: (5, {}), {2}: (6, {}), {3}: (7, {})} | custom-call | flops 40000000 | bytes 8000000 | tf_op jit(solution)/shard_map/side_step/pallas_call | solution.py:797
  15.6 0.0 collective-permute-done.5.rest_10_
  15.7 0.4 %collective-permute-done.6.rest_11_ = f32[4,8,128]{2,1,0:T(8,128)S(1)} collective-permute-done((f32[4,8,128]{2,1,0:T(8,128)S(1)}, f32[4,8,128]{2,1,0:T(8,128)S(1)}, u32[]{:S(2)}, u32[]{:S(2)}) %collective-permute-start.6) | collective-permute-done | bytes 16416 | tf_op jit(solution)/shard_map/ppermute | solution.py:826
  16.1 1.7 %last_steps.1 = (f32[19,8,16,128]{3,2,1,0:T(8,128)}, f32[8,16,128]{2,1,0:T(8,128)}, f32[19,12,32,128]{3,2,1,0:T(8,128)S(1)}, f32[5,10,32,128]{3,2,1,0:T(8,128)S(...) custom-call(f32[2,8,16,128]{3,2,1,0:T(8,128)S(1)} %get-tuple-element, ...), custom_call_target="tpu_custom_call", output_to_operand_aliasing={{2}: (3, {}), {3}: (4, {}), {4}: (5, {}), {5}: (6, {}), {6}... | custom-call | tf_op jit(solution)/shard_map/last_steps/pallas_call | solution.py:797
Async XLA Ops:
  2.5 3.0 %collective-permute-start = (f32[2,16,128]{2,1,0:T(8,128)S(1)}, f32[2,16,128]{2,1,0:T(8,128)S(1)}, u32[]{:S(2)}, u32[]{:S(2)}) collective-permute-start(f32[2,16,128]{2,1,0:T(8,128)S(1)} %get-tuple-element.41), channel_id=1, source_target_pairs={{0,1},{1,0},{2,3},{3,2},{8,9},{9,8},{10,11},{11,10},{16,17},{17,16... | collective-permute-start | bytes 49160 | tf_op jit(solution)/shard_map/ppermute | solution.py:826
  2.6 4.0 %collective-permute-start.1 = (f32[2,16,128]{2,1,0:T(8,128)S(1)}, f32[2,16,128]{2,1,0:T(8,128)S(1)}, u32[]{:S(2)}, u32[]{:S(2)}) collective-permute-start(f32[2,16,128]{2,1,0:T(8,128)S(1)} %get-tuple-element.42), channel_id=1, source_target_pairs={{0,8},{1,2},{2,1},{3,11},{8,0},{9,10},{10,9},{11,3},{16,24},{17,18... | collective-permute-start | bytes 49160 | tf_op jit(solution)/shard_map/ppermute | solution.py:826
  7.2 6.2 %collective-permute-start.2 = (f32[16,16,128]{2,1,0:T(8,128)S(1)}, f32[16,16,128]{2,1,0:T(8,128)S(1)}, u32[]{:S(2)}, u32[]{:S(2)}) collective-permute-start(f32[16,16,128]{2,1,0:T(8,128)S(1)} %get-tuple-element.55), channel_id=1, source_target_pairs={{0,8},{1,9},{2,10},{3,11},{8,0},{9,1},{10,2},{11,3},{16,24},{17,25... | collective-permute-start | bytes 393224 | tf_op jit(solution)/shard_map/ppermute | solution.py:826
  8.7 5.5 %collective-permute-start.3 = (f32[16,16,128]{2,1,0:T(8,128)S(1)}, f32[16,16,128]{2,1,0:T(8,128)S(1)}, u32[]{:S(2)}, u32[]{:S(2)}) collective-permute-start(f32[16,16,128]{2,1,0:T(8,128)S(1)} %get-tuple-element.56), channel_id=1, source_target_pairs={{0,24},{1,25},{2,3},{3,2},{8,16},{9,17},{10,18},{11,19},{16,8},{17... | collective-permute-start | bytes 393224 | tf_op jit(solution)/shard_map/ppermute | solution.py:826
  9.9 3.5 %collective-permute-start.4 = (f32[17,8,128]{2,1,0:T(8,128)S(1)}, f32[17,8,128]{2,1,0:T(8,128)S(1)}, u32[]{:S(2)}, u32[]{:S(2)}) collective-permute-start(f32[17,8,128]{2,1,0:T(8,128)S(1)} %get-tuple-element.57), channel_id=1, source_target_pairs={{0,4},{1,5},{2,6},{3,7},{4,0},{5,1},{6,2},{7,3},{8,12},{9,13},{10,... | collective-permute-start | bytes 208904 | tf_op jit(solution)/shard_map/ppermute | solution.py:826
  11.2 4.5 %collective-permute-start.5 = (f32[4,8,128]{2,1,0:T(8,128)S(1)}, f32[4,8,128]{2,1,0:T(8,128)S(1)}, u32[]{:S(2)}, u32[]{:S(2)}) collective-permute-start(f32[4,8,128]{2,1,0:T(8,128)S(1)} %get-tuple-element.68), channel_id=1, source_target_pairs={{0,12},{4,8},{8,4},{12,0},{16,28},{20,24},{24,20},{28,16},{1,13},{... | collective-permute-start | bytes 49160 | tf_op jit(solution)/shard_map/ppermute | solution.py:826
  12.0 4.1 %collective-permute-start.6 = (f32[4,8,128]{2,1,0:T(8,128)S(1)}, f32[4,8,128]{2,1,0:T(8,128)S(1)}, u32[]{:S(2)}, u32[]{:S(2)}) collective-permute-start(f32[4,8,128]{2,1,0:T(8,128)S(1)} %get-tuple-element.69), channel_id=1, source_target_pairs={{0,4},{4,0},{8,20},{12,16},{16,12},{20,8},{24,28},{28,24},{1,5},{5... | collective-permute-start | bytes 49160 | tf_op jit(solution)/shard_map/ppermute | solution.py:826

commit v4 on v3

--- a/solution.py
+++ b/solution.py
@@ -136,9 +136,9 @@
     packets, sems = rest[:slots], rest[slots]
     refs = (adj, den, vel, mask)
     ext_x, ext_y, _ = mask.shape
-    starts = range(0, 19, 5)
+    starts = range(0, 19, 10)
     loads = [
-        pltpu.make_async_copy(adj_in.at[start : min(start + 5, 19)], adj.at[start : min(start + 5, 19)], sems.at[at])
+        pltpu.make_async_copy(adj_in.at[start : min(start + 10, 19)], adj.at[start : min(start + 10, 19)], sems.at[at])
         for at, start in enumerate(starts)
     ] + [
         pltpu.make_async_copy(source, target, sems.at[len(starts) + at])
@@ -175,7 +175,7 @@
 
     for start, load in zip(starts, loads):
         load.wait()
-        for j in range(start, min(start + 5, 19)):
+        for j in range(start, min(start + 10, 19)):
             gather("pop", j)
     for load in loads[len(starts) :]:
         load.wait()
@@ -834,7 +834,7 @@
             loaded + [array(2, ext_y, LANES)] + [array(2, ext_y, LANES)] * many_z,
             8,
             in_specs=[hbm] * 4,
-            scratch_shapes=[pltpu.SemaphoreType.DMA((7,))],
+            scratch_shapes=[pltpu.SemaphoreType.DMA((5,))],
         ),
         *[None] * (2 - many_z),
     )

time: 17.9 us -> 17.9 us (level)
  no operation moved by 1% of the time
where the time goes in v4:
time: 17.9 us; the launch traced here: 17.7 us
  starting transfers between devices  8.35 us (47%)
  Pallas kernels  6.35 us (35%)
  waiting for transfers between devices  2.32 us (13%)
  between operations  0.69 us (4%)
    ppermute x7, starting transfers between devices, swap(): return lax.ppermute(value, tuple(axes), pairs)  8.35 us
    pallas_call x6, Pallas kernels, call(): pl.pallas_call(kernel, out_shape=shapes, compiler_params=params, name=nam...  6.35 us
    ppermute x7, waiting for transfers between devices, swap(): return lax.ppermute(value, tuple(axes), pairs)  2.32 us
  transfers between devices with their start and end apart: 7, of which 3 were waited for; matrix products, arithmetic and copies ran while one was open for 0% of the time, Pallas kernels for 13%

profile of v4, /device:TPU:9, one launch (start us, length us, event | category | flops | bytes accessed | tf_op | source)
XLA Modules:
  0.0 17.7 jit_solution(10210728902774710766)
XLA Ops:
  0.6 1.8 %pack_z.1 = (f32[19,8,16,128]{3,2,1,0:T(8,128)S(1)}, f32[2,8,16,128]{3,2,1,0:T(8,128)S(1)}, f32[2,3,8,16,128]{4,3,2,1,0:T(8,128)S(1)}, s32[8,16,128]{2,1,0:T(8,1...) custom-call(f32[19,8,16,128]{3,2,1,0:T(8,128)} %adj_in.1, ...), custom_call_target="tpu_custom_call" | custom-call | tf_op jit(solution)/shard_map/pack_z/pallas_call | solution.py:797
  2.5 0.1 collective-permute-start
  2.6 2.6 %collective-permute-start.1 = (f32[2,16,128]{2,1,0:T(8,128)S(1)}, f32[2,16,128]{2,1,0:T(8,128)S(1)}, u32[]{:S(2)}, u32[]{:S(2)}) collective-permute-start(f32[2,16,128]{2,1,0:T(8,128)S(1)} %get-tuple-element.42), channel_id=1, source_target_pairs={{0,8},{1,2},{2,1},{3,11},{8,0},{9,10},{10,9},{11,3},{16,24},{17,18... | collective-permute-start | bytes 49160 | tf_op jit(solution)/shard_map/ppermute | solution.py:826
  5.1 0.4 %shift.1 = (f32[19,12,32,128]{3,2,1,0:T(8,128)S(1)}, f32[16,16,128]{2,1,0:T(8,128)S(1)}, f32[16,16,128]{2,1,0:T(8,128)S(1)}, f32[24,8,128]{2,1,0:T(8,128)S(1)}, ...) custom-call(f32[19,8,16,128]{3,2,1,0:T(8,128)S(1)} %get-tuple-element.43.adj, ...), custom_call_target="tpu_custom_call" | custom-call | flops 1000000 | bytes 2500000 | tf_op jit(solution)/shard_map/shift/pallas_call | solution.py:797
  5.5 0.0 collective-permute-done.rest_0_
  5.5 1.0 %collective-permute-done.1.rest_1_ = f32[2,16,128]{2,1,0:T(8,128)S(1)} collective-permute-done((f32[2,16,128]{2,1,0:T(8,128)S(1)}, f32[2,16,128]{2,1,0:T(8,128)S(1)}, u32[]{:S(2)}, u32[]{:S(2)}) %collective-permute-start.1) | collective-permute-done | bytes 16416 | tf_op jit(solution)/shard_map/ppermute | solution.py:826
  6.6 0.6 %pack_xy.1 = (f32[8,16,128]{2,1,0:T(8,128)S(1)}, f32[19,12,32,128]{3,2,1,0:T(8,128)S(1)}, f32[16,16,128]{2,1,0:T(8,128)S(1)}, f32[16,16,128]{2,1,0:T(8,128)S(1)}...) custom-call(f32[2,8,16,128]{3,2,1,0:T(8,128)S(1)} %get-tuple-element, ...), custom_call_target="tpu_custom_call", output_to_operand_aliasing={{1}: (6, {}), {2}: (7, {}), {3}: (8, {}), {4}: (9, {}), {5}... | custom-call | tf_op jit(solution)/shard_map/pack_xy/pallas_call | solution.py:797
  7.1 1.6 %collective-permute-start.2 = (f32[16,16,128]{2,1,0:T(8,128)S(1)}, f32[16,16,128]{2,1,0:T(8,128)S(1)}, u32[]{:S(2)}, u32[]{:S(2)}) collective-permute-start(f32[16,16,128]{2,1,0:T(8,128)S(1)} %get-tuple-element.55), channel_id=1, source_target_pairs={{0,8},{1,9},{2,10},{3,11},{8,0},{9,1},{10,2},{11,3},{16,24},{17,25... | collective-permute-start | bytes 393224 | tf_op jit(solution)/shard_map/ppermute | solution.py:826
  8.7 1.2 %collective-permute-start.3 = (f32[16,16,128]{2,1,0:T(8,128)S(1)}, f32[16,16,128]{2,1,0:T(8,128)S(1)}, u32[]{:S(2)}, u32[]{:S(2)}) collective-permute-start(f32[16,16,128]{2,1,0:T(8,128)S(1)} %get-tuple-element.56), channel_id=1, source_target_pairs={{0,24},{1,25},{2,3},{3,2},{8,16},{9,17},{10,18},{11,19},{16,8},{17... | collective-permute-start | bytes 393224 | tf_op jit(solution)/shard_map/ppermute | solution.py:826
  9.9 1.2 %collective-permute-start.4 = (f32[17,8,128]{2,1,0:T(8,128)S(1)}, f32[17,8,128]{2,1,0:T(8,128)S(1)}, u32[]{:S(2)}, u32[]{:S(2)}) collective-permute-start(f32[17,8,128]{2,1,0:T(8,128)S(1)} %get-tuple-element.57), channel_id=1, source_target_pairs={{0,4},{1,5},{2,6},{3,7},{4,0},{5,1},{6,2},{7,3},{8,12},{9,13},{10,... | collective-permute-start | bytes 208904 | tf_op jit(solution)/shard_map/ppermute | solution.py:826
  11.1 0.8 %collective-permute-start.5 = (f32[4,8,128]{2,1,0:T(8,128)S(1)}, f32[4,8,128]{2,1,0:T(8,128)S(1)}, u32[]{:S(2)}, u32[]{:S(2)}) collective-permute-start(f32[4,8,128]{2,1,0:T(8,128)S(1)} %get-tuple-element.68), channel_id=1, source_target_pairs={{0,12},{4,8},{8,4},{12,0},{16,28},{20,24},{24,20},{28,16},{1,13},{... | collective-permute-start | bytes 49160 | tf_op jit(solution)/shard_map/ppermute | solution.py:826
  12.0 0.8 %collective-permute-start.6 = (f32[4,8,128]{2,1,0:T(8,128)S(1)}, f32[4,8,128]{2,1,0:T(8,128)S(1)}, u32[]{:S(2)}, u32[]{:S(2)}) collective-permute-start(f32[4,8,128]{2,1,0:T(8,128)S(1)} %get-tuple-element.69), channel_id=1, source_target_pairs={{0,4},{4,0},{8,20},{12,16},{16,12},{20,8},{24,28},{28,24},{1,5},{5... | collective-permute-start | bytes 49160 | tf_op jit(solution)/shard_map/ppermute | solution.py:826
  12.8 0.5 %inner_step.1 = (f32[5,10,32,128]{3,2,1,0:T(8,128)S(1)}, f32[19,10,32,128]{3,2,1,0:T(8,128)S(1)}, f32[1,10,32,128]{3,2,1,0:T(8,128)S(1)}) custom-call(f32[2,8,16,128]{3,2,1,0:T(8,128)S(1)} %get-tuple-element.37.den, f32[2,3,8,16,128]{4,3,2,1,0:T(8,128)S(1)} %get-tuple-element.38.vel, s32[8,16,128]{2,1,0:T(8,128)S(1)} %get-tuple-element.39.mask, ...), custom_call_target="tpu_custom_call" | custom-call | flops 40000000 | bytes 8000000 | tf_op jit(solution)/shard_map/inner_step/pallas_call | solution.py:797
  13.3 0.0 collective-permute-done.4.rest_6_
  13.4 0.0 collective-permute-done.2.rest_4_
  13.4 0.8 %collective-permute-done.3.rest_5_ = f32[16,16,128]{2,1,0:T(8,128)S(1)} collective-permute-done((f32[16,16,128]{2,1,0:T(8,128)S(1)}, f32[16,16,128]{2,1,0:T(8,128)S(1)}, u32[]{:S(2)}, u32[]{:S(2)}) %collective-permute-start.3) | collective-permute-done | bytes 131104 | tf_op jit(solution)/shard_map/ppermute | solution.py:826
  14.2 1.4 %side_step.1 = (f32[19,12,32,128]{3,2,1,0:T(8,128)S(1)}, f32[5,10,32,128]{3,2,1,0:T(8,128)S(1)}, f32[19,10,32,128]{3,2,1,0:T(8,128)S(1)}, f32[1,10,32,128]{3,2,1...) custom-call(f32[2,8,16,128]{3,2,1,0:T(8,128)S(1)} %get-tuple-element, ...), custom_call_target="tpu_custom_call", output_to_operand_aliasing={{0}: (4, {}), {1}: (5, {}), {2}: (6, {}), {3}: (7, {})} | custom-call | flops 40000000 | bytes 8000000 | tf_op jit(solution)/shard_map/side_step/pallas_call | solution.py:797
  15.6 0.0 collective-permute-done.5.rest_10_
  15.6 0.4 %collective-permute-done.6.rest_11_ = f32[4,8,128]{2,1,0:T(8,128)S(1)} collective-permute-done((f32[4,8,128]{2,1,0:T(8,128)S(1)}, f32[4,8,128]{2,1,0:T(8,128)S(1)}, u32[]{:S(2)}, u32[]{:S(2)}) %collective-permute-start.6) | collective-permute-done | bytes 16416 | tf_op jit(solution)/shard_map/ppermute | solution.py:826
  16.1 1.7 %last_steps.1 = (f32[19,8,16,128]{3,2,1,0:T(8,128)}, f32[8,16,128]{2,1,0:T(8,128)}, f32[19,12,32,128]{3,2,1,0:T(8,128)S(1)}, f32[5,10,32,128]{3,2,1,0:T(8,128)S(...) custom-call(f32[2,8,16,128]{3,2,1,0:T(8,128)S(1)} %get-tuple-element, ...), custom_call_target="tpu_custom_call", output_to_operand_aliasing={{2}: (3, {}), {3}: (4, {}), {4}: (5, {}), {5}: (6, {}), {6}... | custom-call | tf_op jit(solution)/shard_map/last_steps/pallas_call | solution.py:797
Async XLA Ops:
  2.5 3.0 %collective-permute-start = (f32[2,16,128]{2,1,0:T(8,128)S(1)}, f32[2,16,128]{2,1,0:T(8,128)S(1)}, u32[]{:S(2)}, u32[]{:S(2)}) collective-permute-start(f32[2,16,128]{2,1,0:T(8,128)S(1)} %get-tuple-element.41), channel_id=1, source_target_pairs={{0,1},{1,0},{2,3},{3,2},{8,9},{9,8},{10,11},{11,10},{16,17},{17,16... | collective-permute-start | bytes 49160 | tf_op jit(solution)/shard_map/ppermute | solution.py:826
  2.6 4.0 %collective-permute-start.1 = (f32[2,16,128]{2,1,0:T(8,128)S(1)}, f32[2,16,128]{2,1,0:T(8,128)S(1)}, u32[]{:S(2)}, u32[]{:S(2)}) collective-permute-start(f32[2,16,128]{2,1,0:T(8,128)S(1)} %get-tuple-element.42), channel_id=1, source_target_pairs={{0,8},{1,2},{2,1},{3,11},{8,0},{9,10},{10,9},{11,3},{16,24},{17,18... | collective-permute-start | bytes 49160 | tf_op jit(solution)/shard_map/ppermute | solution.py:826
  7.1 6.2 %collective-permute-start.2 = (f32[16,16,128]{2,1,0:T(8,128)S(1)}, f32[16,16,128]{2,1,0:T(8,128)S(1)}, u32[]{:S(2)}, u32[]{:S(2)}) collective-permute-start(f32[16,16,128]{2,1,0:T(8,128)S(1)} %get-tuple-element.55), channel_id=1, source_target_pairs={{0,8},{1,9},{2,10},{3,11},{8,0},{9,1},{10,2},{11,3},{16,24},{17,25... | collective-permute-start | bytes 393224 | tf_op jit(solution)/shard_map/ppermute | solution.py:826
  8.7 5.5 %collective-permute-start.3 = (f32[16,16,128]{2,1,0:T(8,128)S(1)}, f32[16,16,128]{2,1,0:T(8,128)S(1)}, u32[]{:S(2)}, u32[]{:S(2)}) collective-permute-start(f32[16,16,128]{2,1,0:T(8,128)S(1)} %get-tuple-element.56), channel_id=1, source_target_pairs={{0,24},{1,25},{2,3},{3,2},{8,16},{9,17},{10,18},{11,19},{16,8},{17... | collective-permute-start | bytes 393224 | tf_op jit(solution)/shard_map/ppermute | solution.py:826
  9.9 3.5 %collective-permute-start.4 = (f32[17,8,128]{2,1,0:T(8,128)S(1)}, f32[17,8,128]{2,1,0:T(8,128)S(1)}, u32[]{:S(2)}, u32[]{:S(2)}) collective-permute-start(f32[17,8,128]{2,1,0:T(8,128)S(1)} %get-tuple-element.57), channel_id=1, source_target_pairs={{0,4},{1,5},{2,6},{3,7},{4,0},{5,1},{6,2},{7,3},{8,12},{9,13},{10,... | collective-permute-start | bytes 208904 | tf_op jit(solution)/shard_map/ppermute | solution.py:826
  11.1 4.5 %collective-permute-start.5 = (f32[4,8,128]{2,1,0:T(8,128)S(1)}, f32[4,8,128]{2,1,0:T(8,128)S(1)}, u32[]{:S(2)}, u32[]{:S(2)}) collective-permute-start(f32[4,8,128]{2,1,0:T(8,128)S(1)} %get-tuple-element.68), channel_id=1, source_target_pairs={{0,12},{4,8},{8,4},{12,0},{16,28},{20,24},{24,20},{28,16},{1,13},{... | collective-permute-start | bytes 49160 | tf_op jit(solution)/shard_map/ppermute | solution.py:826
  12.0 4.1 %collective-permute-start.6 = (f32[4,8,128]{2,1,0:T(8,128)S(1)}, f32[4,8,128]{2,1,0:T(8,128)S(1)}, u32[]{:S(2)}, u32[]{:S(2)}) collective-permute-start(f32[4,8,128]{2,1,0:T(8,128)S(1)} %get-tuple-element.69), channel_id=1, source_target_pairs={{0,4},{4,0},{8,20},{12,16},{16,12},{20,8},{24,28},{28,24},{1,5},{5... | collective-permute-start | bytes 49160 | tf_op jit(solution)/shard_map/ppermute | solution.py:826
